TPU v7x, 128 devices: a whole 4x4x4 slice. The times are simulated.
128 devices in a mesh: ctx: 32 (over y, x, core), head: 4 (over z).
Axes of the slice: x: 4, y: 4, z: 4, core: 2. Of those that a mesh axis runs over, the one named last changes fastest.
Arguments:
- prefix: bfloat16 [262144, 1024], P(('ctx', 'head')), may hold values from -6 to 6
- keep_blocks: int32 [4, 32, 16], P('head', 'ctx'), may hold values from 0 to 15, each once within a row
- keep_count: int32 [4, 32], P('head', 'ctx'), may hold values from 1 to 16, 256 in all within a row
- latent_inputs: bfloat16 [512, 1024], P('ctx'), may hold values from -6 to 6
- latent_pos: int32 [512], replicated, may hold values from 0 to 262143
- w_query: bfloat16 [1024, 1024], P(None, 'head')
- w_key: bfloat16 [1024, 1024], replicated, may hold values from -0.1875 to 0.1875
- w_value: bfloat16 [1024, 1024], replicated, may hold values from -0.1875 to 0.1875
Outputs:
- attended: bfloat16 [512, 1024], P('ctx', 'head')
Inputs may be any that keep to these rules, and one draw needn't show every extreme that they name: keep_blocks[h, c, :] lists each of the 16 block numbers once; the first keep_count[h, c] entries are the kept blocks. For every index h, keep_count[h, :] sums to 256, and its largest entry is 16.
All inputs are finite; a program needn't handle non-finite values. No bound on the sum of `keep_count` on one device may be relied on, other than what follows from the above.
Results may differ from a plain program's by a relative error of at most 0.0085.
The roundings to bfloat16 on the way count: a program that leaves them out, or rounds other values in their place, can miss the bound.
Values may be sent and summed in bfloat16 or wider, within the bound.
A program may use at most 128 MiB of HBM per device.

v0:
```python
import math

import jax
import jax.numpy as jnp
from jax import lax
from jax.sharding import PartitionSpec as P

HD = 64
BLOCK = 128


NEG_FILL = -1e30
EPSILON = 1e-06
QUERY_ROWS = 1024


def copy_for_each(array, axis):
    copies = jnp.broadcast_to(array, (lax.axis_size(axis), *array.shape))
    return lax.all_to_all(copies, axis, split_axis=0, concat_axis=0, tiled=True)


def joined_along(pieces, dim):
    dims = list(pieces.shape[1:])
    dims[dim] *= pieces.shape[0]
    return jnp.moveaxis(pieces, 0, dim).reshape(dims)


def gathered_copies(array, axis, dim):
    pieces = copy_for_each(array, axis)
    return joined_along(pieces, dim)


def side_by_side(arrays, axis, dim, along):
    widths = [math.prod(a.shape[along:]) for a in arrays]
    both = jnp.concatenate(
        [a.reshape(*a.shape[:along], w) for a, w in zip(arrays, widths)], axis=along
    )
    whole = lax.all_gather(both, axis, axis=dim, tiled=True)
    pieces = jnp.split(whole, [sum(widths[:k]) for k in range(1, len(widths))], axis=along)
    return tuple(
        (b.reshape(*whole.shape[:along], *a.shape[along:]) for a, b in zip(arrays, pieces))
    )


def sent_together(arrays, axis, split_dim, concat_dim, along):
    widths = [a.shape[along] for a in arrays]
    both = jnp.concatenate(arrays, axis=along)
    whole = lax.all_to_all(both, axis, split_axis=split_dim, concat_axis=concat_dim, tiled=True)
    return tuple(jnp.split(whole, [sum(widths[:k]) for k in range(1, len(widths))], axis=along))


def of_everyone(array, axis):
    everything = copy_for_each(array, axis)
    return jnp.max(everything, axis=0)


def cut_along(array, dim, peers):
    before, after = (array.shape[:dim], array.shape[dim + 1 :])
    return jnp.moveaxis(array.reshape(*before, peers, -1, *after), dim, 0)


def sum_at_owner(array, axis, dim):
    peers = lax.axis_size(axis)
    pieces = lax.all_to_all(cut_along(array, dim, peers), axis, 0, 0, tiled=True)
    return jnp.sum(pieces.astype(jnp.float32), axis=0)


def sent_together_2(arrays, axis, dim, along):
    ends, at = ([], 0)
    for a in arrays[:-1]:
        at += a.shape[along]
        ends.append(at)
    both = jnp.concatenate(arrays, axis=along)
    return tuple(jnp.split(sum_at_owner(both, axis, dim), ends, axis=along))


def normalize(source_rows):
    wide_rows = source_rows.astype(jnp.float32)
    factor = lax.rsqrt(jnp.mean(wide_rows * wide_rows, axis=-1, keepdims=True) + EPSILON)
    return (wide_rows * factor).astype(jnp.bfloat16)


def widen(per_head):
    return jnp.repeat(per_head, HD, axis=1)


def local_partials(queries, key_rows, value_rows, key_pos, key_valid, query_pos):
    key_count = key_rows.shape[0]
    heads_here = queries.shape[1] // HD
    latents = queries.shape[0]
    block_rows = min(QUERY_ROWS, latents)
    block_count = latents // block_rows
    key_heads = key_rows.reshape(key_count, heads_here, HD).transpose(1, 0, 2)
    value_heads = value_rows.reshape(key_count, heads_here, HD).transpose(1, 0, 2)
    query_heads = queries.reshape(block_count, block_rows, heads_here, HD).transpose(2, 0, 1, 3)
    pos_blocks = query_pos.reshape(block_count, block_rows)

    def per_head(head_args):
        key_head, value_head, query_head = head_args

        def per_block(block_args):
            query_block, pos_block = block_args
            scores = jnp.einsum(
                "qd,kd->qk", query_block, key_head, preferred_element_type=jnp.float32
            )
            allowed = key_valid[None, :] & (key_pos[None, :] < pos_block[:, None])
            masked = jnp.where(allowed, scores, NEG_FILL)
            row_top = jnp.max(masked, axis=1)
            weights = jnp.where(allowed, jnp.exp(masked - row_top[:, None]), 0.0)
            weight_sum = jnp.sum(weights, axis=1)
            weighted = jnp.dot(
                weights.astype(jnp.bfloat16), value_head, preferred_element_type=jnp.float32
            )
            return (row_top, weight_sum, weighted)

        return lax.map(per_block, (query_head, pos_blocks))

    row_tops, row_sums, weighted = lax.map(per_head, (key_heads, value_heads, query_heads))
    row_tops = row_tops.transpose(1, 2, 0).reshape(latents, heads_here)
    row_sums = row_sums.transpose(1, 2, 0).reshape(latents, heads_here)
    weighted = weighted.transpose(1, 2, 0, 3).reshape(latents, heads_here * HD)
    return (row_tops, row_sums, weighted)


def per_device(prefix, keep_blocks, keep_count, latent_inputs, latent_pos, w_query, w_key, w_value):
    head_count = lax.axis_size("head")
    ctx_index = lax.axis_index("ctx")
    head_index = lax.axis_index("head")
    block_total = keep_blocks.shape[2]
    head_width = w_query.shape[1]
    own_list = keep_blocks.reshape(1, block_total)
    own_count = keep_count.reshape(1)
    block_range = jnp.arange(block_total, dtype=jnp.int32)
    head_range = jnp.arange(head_count, dtype=jnp.int32)
    normed = normalize(prefix)
    row_count = prefix.shape[0]
    key_local = jnp.dot(normed, w_key, preferred_element_type=jnp.float32).astype(jnp.bfloat16)
    value_local = jnp.dot(normed, w_value, preferred_element_type=jnp.float32).astype(jnp.bfloat16)
    latent_normed = normalize(latent_inputs)
    latent_rows = latent_inputs.shape[0]
    heads_here = head_width // HD
    query_local = (
        jnp.dot(latent_normed, w_query, preferred_element_type=jnp.float32) * HD ** (-0.5)
    ).astype(jnp.bfloat16)
    own_key_cols = lax.dynamic_slice_in_dim(w_key, head_index * head_width, head_width, 1)
    own_value_cols = lax.dynamic_slice_in_dim(w_value, head_index * head_width, head_width, 1)
    self_key = jnp.dot(latent_normed, own_key_cols, preferred_element_type=jnp.float32).astype(
        jnp.bfloat16
    )
    self_value = jnp.dot(latent_normed, own_value_cols, preferred_element_type=jnp.float32).astype(
        jnp.bfloat16
    )
    self_score = jnp.sum(
        (query_local.astype(jnp.float32) * self_key.astype(jnp.float32)).reshape(
            latent_rows, heads_here, HD
        ),
        axis=2,
    )
    all_queries = gathered_copies(query_local, "ctx", 0)
    own_first = ctx_index * latent_rows
    group_list, group_count = side_by_side((own_list, own_count), "head", 0, 1)
    group_match = (group_list[:, :, None] == block_range[None, None, :]) & (
        block_range[None, :, None] < group_count[:, None, None]
    )
    valid_grid = jnp.repeat(jnp.any(group_match, axis=1), BLOCK, axis=1)
    shard_number = ctx_index * head_count + head_range
    pos_grid = (
        shard_number[:, None] * (block_total * BLOCK)
        + jnp.arange(block_total * BLOCK, dtype=jnp.int32)[None, :]
    )
    key_pos = pos_grid.reshape(-1)
    key_valid = valid_grid.reshape(-1)
    key_parts, value_parts = sent_together(
        (
            key_local.reshape(row_count, head_count, head_width),
            value_local.reshape(row_count, head_count, head_width),
        ),
        "head",
        1,
        0,
        2,
    )
    key_rows = key_parts.reshape(head_count * row_count, head_width)
    value_rows = value_parts.reshape(head_count * row_count, head_width)
    row_tops, row_sums, weighted = local_partials(
        all_queries, key_rows, value_rows, key_pos, key_valid, latent_pos
    )
    self_full = lax.dynamic_update_slice(
        jnp.full(row_tops.shape, NEG_FILL, jnp.float32), self_score, (own_first, 0)
    )
    global_top = of_everyone(jnp.maximum(row_tops, self_full), "ctx")
    rescale = jnp.exp(row_tops - global_top)
    share_weighted, share_sums = sent_together_2(
        (
            (weighted * widen(rescale)).astype(jnp.bfloat16),
            (row_sums * rescale).astype(jnp.bfloat16),
        ),
        "ctx",
        0,
        1,
    )
    own_top = lax.dynamic_slice_in_dim(global_top, own_first, latent_rows, 0)
    self_weight = jnp.exp(self_score - own_top)
    denominator = share_sums + self_weight
    numerator = share_weighted + widen(self_weight) * self_value.astype(jnp.float32)
    return (numerator / widen(denominator)).astype(jnp.bfloat16)


def solution(mesh):
    return jax.shard_map(
        per_device,
        mesh=mesh,
        in_specs=(
            P(("ctx", "head"), None),
            P("head", "ctx", None),
            P("head", "ctx"),
            P("ctx", None),
            P(),
            P(None, "head"),
            P(),
            P(),
        ),
        out_specs=P("ctx", "head"),
        check_vma=False,
    )
```

profile of v0, /device:TPU:1, one launch (start us, length us, event | category | flops | bytes accessed | tf_op | source)
XLA Modules:
  0.0 321.4 jit_solution(11519802292835764243)
XLA Ops:
  0.0 1.0 fusion.41
  1.0 1.3 fusion.31
  2.3 0.7 broadcast_in_dim.65
  3.0 8.6 %all-to-all-start = ((bf16[32,16,256]{2,1,0:T(8,128)(2,1)}), bf16[32,16,256]{2,1,0:T(8,128)(2,1)S(1)}, u32[]{:S(2)}, u32[]{:S(2)}) async-start(bf16[32,16,256]{2,1,0:T(8,128)(2,1)} %broadcast_in_dim.65), calls=%async_computation | async-start | bytes 524288 | tf_op jit(solution)/shard_map/all_to_all | solution.py:19
  11.7 3.2 %fusion.27 = f32[2048]{0:T(1024)S(1)} fusion(bf16[2048,1024]{1,0:T(8,128)(2,1)} %param.10), kind=kLoop, calls=%fused_computation.26 | loop fusion | flops 6289408 | bytes 4202496 | tf_op jit(solution)/shard_map/reduce_sum | solution.py:79
  14.9 0.2 copy-done.3
  15.1 8.2 %convolution_convert_fusion = bf16[2048,1024]{0,1:T(8,128)(2,1)} fusion(bf16[1024,1024]{1,0:T(8,128)(2,1)} %param.17, bf16[2048,1024]{1,0:T(8,128)(2,1)S(1)} %copy-done.3, f32[2048]{0:T(1024)S(1)} %add_rsqrt_fusion), kind=kOutput, calls=%fused_computation.29 | convolution fusion | flops 4303355904 | bytes 10493952 | tf_op jit(solution)/shard_map/dot_general | solution.py:138
  23.3 6.2 %copy.80 = bf16[2048,4,256]{2,0,1:T(8,128)(2,1)} copy(bf16[2048,4,256]{0,2,1:T(8,128)(2,1)} %bitcast.90) | data formatting | bytes 8388608 | tf_op jit(solution)/shard_map/reshape | solution.py:176
  29.5 8.7 %convolution_convert_fusion.1 = bf16[2048,1024]{0,1:T(8,128)(2,1)} fusion(bf16[1024,1024]{1,0:T(8,128)(2,1)S(1)} %copy-done, bf16[2048,1024]{1,0:T(8,128)(2,1)} %param.10, f32[2048]{0:T(1024)S(1)} %add_rsqrt_fusion), kind=kOutput, calls=%fused_computation.30 | convolution fusion | flops 4303355904 | bytes 10493952 | tf_op jit(solution)/shard_map/dot_general | solution.py:137
  38.2 6.2 %copy.79 = bf16[2048,4,256]{2,0,1:T(8,128)(2,1)} copy(bf16[2048,4,256]{0,2,1:T(8,128)(2,1)} %bitcast.89) | data formatting | bytes 8388608 | tf_op jit(solution)/shard_map/reshape | solution.py:175
  44.4 7.3 %pad_maximum_fusion = bf16[2048,4,512]{2,0,1:T(8,128)(2,1)} fusion(bf16[2048,4,256]{2,0,1:T(8,128)(2,1)} %copy.80, bf16[2048,4,256]{2,0,1:T(8,128)(2,1)} %copy.79), kind=kLoop, calls=%fused_computation.28 | loop fusion | flops 16777216 | bytes 16777216 | tf_op jit(solution)/shard_map/concatenate | solution.py:47
  51.7 5.8 %all-to-all-start.1 = ((bf16[2048,4,512]{2,0,1:T(8,128)(2,1)}), bf16[2048,4,512]{2,0,1:T(8,128)(2,1)}, u32[]{:S(2)}, u32[]{:S(2)}) async-start(bf16[2048,4,512]{2,0,1:T(8,128)(2,1)} %pad_maximum_fusion), calls=%async_computation.1 | async-start | bytes 16777216 | tf_op jit(solution)/shard_map/all_to_all | solution.py:48
  58.3 0.2 fusion.38
  58.8 0.2 dynamic_update_slice.22
  59.0 94.4 %all-gather = s32[4,1,17]{2,1,0:T(1,128)S(1)} all-gather(s32[1,1,17]{2,1,0:T(1,128)S(1)} %add_bitcast_fusion.1), channel_id=1, replica_groups=mesh['ctx'=32,'head'=4] {'head'}, dimensions={0}, use_global_device_ids=true | all-gather | bytes 340 | tf_op jit(solution)/shard_map/all_gather | solution.py:38
  153.5 0.2 slice_reduce_fusion
  153.7 0.1 fusion.44
  153.8 0.2 reshape_reshape.9
  154.2 5.7 %fusion.51 = (bf16[8192,1,256]{2,0,1:T(8,128)(2,1)}, bf16[8192,1,256]{2,0,1:T(8,128)(2,1)}) fusion(bf16[8192,1,512]{2,0,1:T(8,128)(2,1)} %bitcast.6), kind=kLoop, calls=%fused_computation.70 | loop fusion | bytes 16777216 | tf_op jit(solution)/shard_map/split | solution.py:49
  159.9 6.4 %copy.81 = bf16[8192,1,256]{0,2,1:T(8,128)(2,1)} copy(bf16[8192,1,256]{2,0,1:T(8,128)(2,1)} %get-tuple-element.202) | data formatting | bytes 8388608 | tf_op jit(solution)/shard_map/split | solution.py:49
  166.3 6.4 %copy.82 = bf16[8192,1,256]{0,2,1:T(8,128)(2,1)} copy(bf16[8192,1,256]{2,0,1:T(8,128)(2,1)} %get-tuple-element.201) | data formatting | bytes 8388608 | tf_op jit(solution)/shard_map/split | solution.py:49
  172.6 107.9 %while.15 = (s32[]{:T(128)}, f32[4,1,512]{2,0,1:T(4,128)S(1)}, f32[4,1,512]{2,1,0:T(1,128)S(1)}, f32[4,1,512,64]{2,3,1,0:T(8,128)}, s32[1,512]{1,0:T(1,128)S(1)}...) while((s32[]{:T(128)}, f32[4,1,512]{2,0,1:T(4,128)S(1)}, ...), condition=%wide.region_6.7_spmd.clone, body=%wide.region_3.6_spmd.clone.sunk | while | flops 1140857856 | bytes 120054000 | solution.py:118
  172.8 9.0 %fusion.62 = (f32[512]{0:T(512)S(1)}, f32[512,8192]{1,0:T(8,128)}) fusion(s32[8192]{0:T(1024)S(1)} %bitcast.91, s32[512]{0:T(512)S(1)} %bitcast.103, pred[8192]{0:T(1024)(128)(4,1)S(1)} %bitcast.95, bf16[4,8192,64]{1,2,0:T(8,128)(2,1)} %get-tuple-element.298, s32[]{:T(128)S(6)} %copy.114, bf16[4,1,512,64]{3,2,1,0:T(8,128)(2,1)S(1)} %get-tuple-element.297), kind=kOutput, calls=%fused_computation.5.clone.1 | convolution fusion | flops 553647616 | bytes 18002944 | tf_op jit(solution)/shard_map/while/body/eval_jaxpr/while/body/eval_jaxpr/qd,kd->qk/dot_general | solution.py:103
  181.8 10.6 %fusion.63 = f32[512]{0:T(512)S(1)} fusion(f32[512,8192]{1,0:T(8,128)} %get-tuple-element.267, f32[512]{0:T(512)S(1)} %get-tuple-element.266, s32[8192]{0:T(1024)S(1)} %bitcast.92, s32[512]{0:T(512)S(1)} %bitcast.104, pred[8192]{0:T(1024)(128)(4,1)S(1)} %bitcast.96), kind=kLoop, calls=%fused_computation.7.clone.1 | loop fusion | flops 25165312 | bytes 16824320 | tf_op jit(solution)/shard_map/while/body/eval_jaxpr/while/body/eval_jaxpr/reduce_sum | solution.py:110
  192.5 7.1 %fusion.64 = f32[4,1,512,64]{2,3,1,0:T(8,128)} fusion(f32[4,1,512,64]{2,3,1,0:T(8,128)} %get-tuple-element.283, s32[]{:T(128)S(6)} %copy.114, f32[512,8192]{1,0:T(8,128)S(1)} %copy-done.2, f32[512]{0:T(512)S(1)} %get-tuple-element.266, s32[8192]{0:T(1024)S(1)} %bitcast.93, s32[512]{0:T(512)S(1)} %bitcast.105, pred[8192]{0:T(1024)(128)(4,1)S(1)} %bitcast.97, ...), kind=kOutput, calls=%fused_computation.10.clone.1 | convolution fusion | flops 562036736 | bytes 18002944 | tf_op jit(solution)/shard_map/while/body/eval_jaxpr/while/body/eval_jaxpr/dot_general | solution.py:111
  199.8 9.0 %fusion.62 = (f32[512]{0:T(512)S(1)}, f32[512,8192]{1,0:T(8,128)}) fusion(s32[8192]{0:T(1024)S(1)} %bitcast.91, s32[512]{0:T(512)S(1)} %bitcast.103, pred[8192]{0:T(1024)(128)(4,1)S(1)} %bitcast.95, bf16[4,8192,64]{1,2,0:T(8,128)(2,1)} %get-tuple-element.298, s32[]{:T(128)S(6)} %copy.114, bf16[4,1,512,64]{3,2,1,0:T(8,128)(2,1)S(1)} %get-tuple-element.297), kind=kOutput, calls=%fused_computation.5.clone.1 | convolution fusion | flops 553647616 | bytes 18002944 | tf_op jit(solution)/shard_map/while/body/eval_jaxpr/while/body/eval_jaxpr/qd,kd->qk/dot_general | solution.py:103
  208.8 10.6 %fusion.63 = f32[512]{0:T(512)S(1)} fusion(f32[512,8192]{1,0:T(8,128)} %get-tuple-element.267, f32[512]{0:T(512)S(1)} %get-tuple-element.266, s32[8192]{0:T(1024)S(1)} %bitcast.92, s32[512]{0:T(512)S(1)} %bitcast.104, pred[8192]{0:T(1024)(128)(4,1)S(1)} %bitcast.96), kind=kLoop, calls=%fused_computation.7.clone.1 | loop fusion | flops 25165312 | bytes 16824320 | tf_op jit(solution)/shard_map/while/body/eval_jaxpr/while/body/eval_jaxpr/reduce_sum | solution.py:110
  219.5 7.1 %fusion.64 = f32[4,1,512,64]{2,3,1,0:T(8,128)} fusion(f32[4,1,512,64]{2,3,1,0:T(8,128)} %get-tuple-element.283, s32[]{:T(128)S(6)} %copy.114, f32[512,8192]{1,0:T(8,128)S(1)} %copy-done.2, f32[512]{0:T(512)S(1)} %get-tuple-element.266, s32[8192]{0:T(1024)S(1)} %bitcast.93, s32[512]{0:T(512)S(1)} %bitcast.105, pred[8192]{0:T(1024)(128)(4,1)S(1)} %bitcast.97, ...), kind=kOutput, calls=%fused_computation.10.clone.1 | convolution fusion | flops 562036736 | bytes 18002944 | tf_op jit(solution)/shard_map/while/body/eval_jaxpr/while/body/eval_jaxpr/dot_general | solution.py:111
  226.8 9.0 %fusion.62 = (f32[512]{0:T(512)S(1)}, f32[512,8192]{1,0:T(8,128)}) fusion(s32[8192]{0:T(1024)S(1)} %bitcast.91, s32[512]{0:T(512)S(1)} %bitcast.103, pred[8192]{0:T(1024)(128)(4,1)S(1)} %bitcast.95, bf16[4,8192,64]{1,2,0:T(8,128)(2,1)} %get-tuple-element.298, s32[]{:T(128)S(6)} %copy.114, bf16[4,1,512,64]{3,2,1,0:T(8,128)(2,1)S(1)} %get-tuple-element.297), kind=kOutput, calls=%fused_computation.5.clone.1 | convolution fusion | flops 553647616 | bytes 18002944 | tf_op jit(solution)/shard_map/while/body/eval_jaxpr/while/body/eval_jaxpr/qd,kd->qk/dot_general | solution.py:103
  235.8 10.6 %fusion.63 = f32[512]{0:T(512)S(1)} fusion(f32[512,8192]{1,0:T(8,128)} %get-tuple-element.267, f32[512]{0:T(512)S(1)} %get-tuple-element.266, s32[8192]{0:T(1024)S(1)} %bitcast.92, s32[512]{0:T(512)S(1)} %bitcast.104, pred[8192]{0:T(1024)(128)(4,1)S(1)} %bitcast.96), kind=kLoop, calls=%fused_computation.7.clone.1 | loop fusion | flops 25165312 | bytes 16824320 | tf_op jit(solution)/shard_map/while/body/eval_jaxpr/while/body/eval_jaxpr/reduce_sum | solution.py:110
  246.5 7.1 %fusion.64 = f32[4,1,512,64]{2,3,1,0:T(8,128)} fusion(f32[4,1,512,64]{2,3,1,0:T(8,128)} %get-tuple-element.283, s32[]{:T(128)S(6)} %copy.114, f32[512,8192]{1,0:T(8,128)S(1)} %copy-done.2, f32[512]{0:T(512)S(1)} %get-tuple-element.266, s32[8192]{0:T(1024)S(1)} %bitcast.93, s32[512]{0:T(512)S(1)} %bitcast.105, pred[8192]{0:T(1024)(128)(4,1)S(1)} %bitcast.97, ...), kind=kOutput, calls=%fused_computation.10.clone.1 | convolution fusion | flops 562036736 | bytes 18002944 | tf_op jit(solution)/shard_map/while/body/eval_jaxpr/while/body/eval_jaxpr/dot_general | solution.py:111
  253.7 9.0 %fusion.62 = (f32[512]{0:T(512)S(1)}, f32[512,8192]{1,0:T(8,128)}) fusion(s32[8192]{0:T(1024)S(1)} %bitcast.91, s32[512]{0:T(512)S(1)} %bitcast.103, pred[8192]{0:T(1024)(128)(4,1)S(1)} %bitcast.95, bf16[4,8192,64]{1,2,0:T(8,128)(2,1)} %get-tuple-element.298, s32[]{:T(128)S(6)} %copy.114, bf16[4,1,512,64]{3,2,1,0:T(8,128)(2,1)S(1)} %get-tuple-element.297), kind=kOutput, calls=%fused_computation.5.clone.1 | convolution fusion | flops 553647616 | bytes 18002944 | tf_op jit(solution)/shard_map/while/body/eval_jaxpr/while/body/eval_jaxpr/qd,kd->qk/dot_general | solution.py:103
  262.8 10.6 %fusion.63 = f32[512]{0:T(512)S(1)} fusion(f32[512,8192]{1,0:T(8,128)} %get-tuple-element.267, f32[512]{0:T(512)S(1)} %get-tuple-element.266, s32[8192]{0:T(1024)S(1)} %bitcast.92, s32[512]{0:T(512)S(1)} %bitcast.104, pred[8192]{0:T(1024)(128)(4,1)S(1)} %bitcast.96), kind=kLoop, calls=%fused_computation.7.clone.1 | loop fusion | flops 25165312 | bytes 16824320 | tf_op jit(solution)/shard_map/while/body/eval_jaxpr/while/body/eval_jaxpr/reduce_sum | solution.py:110
  273.5 7.1 %fusion.64 = f32[4,1,512,64]{2,3,1,0:T(8,128)} fusion(f32[4,1,512,64]{2,3,1,0:T(8,128)} %get-tuple-element.283, s32[]{:T(128)S(6)} %copy.114, f32[512,8192]{1,0:T(8,128)S(1)} %copy-done.2, f32[512]{0:T(512)S(1)} %get-tuple-element.266, s32[8192]{0:T(1024)S(1)} %bitcast.93, s32[512]{0:T(512)S(1)} %bitcast.105, pred[8192]{0:T(1024)(128)(4,1)S(1)} %bitcast.97, ...), kind=kOutput, calls=%fused_computation.10.clone.1 | convolution fusion | flops 562036736 | bytes 18002944 | tf_op jit(solution)/shard_map/while/body/eval_jaxpr/while/body/eval_jaxpr/dot_general | solution.py:111
  280.6 0.7 broadcast_in_dim.67
  281.3 8.5 %all-to-all-start.2 = ((f32[32,512,4]{1,2,0:T(4,128)}), f32[32,512,4]{1,2,0:T(4,128)S(1)}, u32[]{:S(2)}, u32[]{:S(2)}) async-start(f32[32,512,4]{1,2,0:T(4,128)} %broadcast_in_dim.67), calls=%async_computation.2 | async-start | bytes 524288 | tf_op jit(solution)/shard_map/all_to_all | solution.py:19
  290.2 1.4 copy.86
  291.6 1.4 reshape.106
  293.1 5.7 %all-to-all-done.2 = f32[32,512,4]{1,2,0:T(4,128)S(1)} async-done(((f32[32,512,4]{1,2,0:T(4,128)}), f32[32,512,4]{1,2,0:T(4,128)S(1)}, u32[]{:S(2)}, u32[]{:S(2)}) %all-to-all-start.2) | async-done | bytes 262176 | tf_op jit(solution)/shard_map/all_to_all | solution.py:19
  299.0 0.8 copy.93
  299.8 0.1 copy.89
  300.0 0.6 broadcast_in_dim.68
  300.6 1.4 reshape.109
  302.0 1.3 multiply_convert_fusion
  303.3 1.7 pad_maximum_fusion.1
  305.0 3.8 %all-to-all-start.3 = ((bf16[32,16,260]{2,1,0:T(8,128)(2,1)}), bf16[32,16,260]{2,1,0:T(8,128)(2,1)S(1)}, u32[]{:S(2)}, u32[]{:S(2)}) async-start(bf16[32,16,260]{2,1,0:T(8,128)(2,1)} %pad_maximum_fusion.1), calls=%async_computation.3 | async-start | bytes 786432 | tf_op jit(solution)/shard_map/all_to_all | solution.py:64
  308.9 10.1 %all-to-all-done.3 = bf16[32,16,260]{2,1,0:T(8,128)(2,1)S(1)} async-done(((bf16[32,16,260]{2,1,0:T(8,128)(2,1)}), bf16[32,16,260]{2,1,0:T(8,128)(2,1)S(1)}, u32[]{:S(2)}, u32[]{:S(2)}) %all-to-all-start.3) | async-done | bytes 266272 | tf_op jit(solution)/shard_map/all_to_all | solution.py:64
  319.5 1.9 fusion.36
  (73 shorter events, 2.7 us)
Async XLA Ops:
  0.0 29.5 %copy-start = (bf16[1024,1024]{1,0:T(8,128)(2,1)S(1)}, bf16[1024,1024]{1,0:T(8,128)(2,1)}, u32[]{:S(2)}) copy-start(bf16[1024,1024]{1,0:T(8,128)(2,1)} %param.16) | copy-start | bytes 6291460
  3.0 48.7 %all-to-all-start = ((bf16[32,16,256]{2,1,0:T(8,128)(2,1)}), bf16[32,16,256]{2,1,0:T(8,128)(2,1)S(1)}, u32[]{:S(2)}, u32[]{:S(2)}) async-start(bf16[32,16,256]{2,1,0:T(8,128)(2,1)} %broadcast_in_dim.65), calls=%async_computation | async-start | bytes 524288 | tf_op jit(solution)/shard_map/all_to_all | solution.py:19
  11.6 3.5 %copy-start.3 = (bf16[2048,1024]{1,0:T(8,128)(2,1)S(1)}, bf16[2048,1024]{1,0:T(8,128)(2,1)}, u32[]{:S(2)}) copy-start(bf16[2048,1024]{1,0:T(8,128)(2,1)} %param.10) | copy-start | bytes 12582916
  51.7 6.5 %copy-start.4 = (bf16[16,1024]{1,0:T(8,128)(2,1)S(1)}, bf16[16,1024]{1,0:T(8,128)(2,1)}, u32[]{:S(2)}) copy-start(bf16[16,1024]{1,0:T(8,128)(2,1)} %param.13) | copy-start | bytes 98308
  51.7 7.2 %copy-start.6 = (s32[1,1,16]{2,1,0:T(1,128)S(1)}, s32[1,1,16]{2,1,0:T(1,128)}, u32[]{:S(2)}) copy-start(s32[1,1,16]{2,1,0:T(1,128)} %param.11) | copy-start | bytes 196
  51.7 102.4 %all-to-all-start.1 = ((bf16[2048,4,512]{2,0,1:T(8,128)(2,1)}), bf16[2048,4,512]{2,0,1:T(8,128)(2,1)}, u32[]{:S(2)}, u32[]{:S(2)}) async-start(bf16[2048,4,512]{2,0,1:T(8,128)(2,1)} %pad_maximum_fusion), calls=%async_computation.1 | async-start | bytes 16777216 | tf_op jit(solution)/shard_map/all_to_all | solution.py:48
  166.3 6.4 %copy-start.5 = (s32[512]{0:T(512)S(1)}, s32[512]{0:T(512)}, u32[]{:S(2)}) copy-start(s32[512]{0:T(512)} %param.14) | copy-start | bytes 6148
  181.8 10.7 %copy-start.2 = (f32[512,8192]{1,0:T(8,128)S(1)}, f32[512,8192]{1,0:T(8,128)}, u32[]{:S(2)}) copy-start(f32[512,8192]{1,0:T(8,128)} %get-tuple-element.267) | copy-start | bytes 50331652 | tf_op jit(solution)/shard_map/while
  208.8 10.7 %copy-start.2 = (f32[512,8192]{1,0:T(8,128)S(1)}, f32[512,8192]{1,0:T(8,128)}, u32[]{:S(2)}) copy-start(f32[512,8192]{1,0:T(8,128)} %get-tuple-element.267) | copy-start | bytes 50331652 | tf_op jit(solution)/shard_map/while
  235.8 10.7 %copy-start.2 = (f32[512,8192]{1,0:T(8,128)S(1)}, f32[512,8192]{1,0:T(8,128)}, u32[]{:S(2)}) copy-start(f32[512,8192]{1,0:T(8,128)} %get-tuple-element.267) | copy-start | bytes 50331652 | tf_op jit(solution)/shard_map/while
  262.8 10.7 %copy-start.2 = (f32[512,8192]{1,0:T(8,128)S(1)}, f32[512,8192]{1,0:T(8,128)}, u32[]{:S(2)}) copy-start(f32[512,8192]{1,0:T(8,128)} %get-tuple-element.267) | copy-start | bytes 50331652 | tf_op jit(solution)/shard_map/while
  281.3 17.4 %all-to-all-start.2 = ((f32[32,512,4]{1,2,0:T(4,128)}), f32[32,512,4]{1,2,0:T(4,128)S(1)}, u32[]{:S(2)}, u32[]{:S(2)}) async-start(f32[32,512,4]{1,2,0:T(4,128)} %broadcast_in_dim.67), calls=%async_computation.2 | async-start | bytes 524288 | tf_op jit(solution)/shard_map/all_to_all | solution.py:19
  291.6 29.7 %copy-start.1 = (bf16[1024,1024]{1,0:T(8,128)(2,1)S(1)}, bf16[1024,1024]{1,0:T(8,128)(2,1)}, u32[]{:S(2)}) copy-start(bf16[1024,1024]{1,0:T(8,128)(2,1)} %param.16) | copy-start | bytes 6291460
  305.0 14.1 %all-to-all-start.3 = ((bf16[32,16,260]{2,1,0:T(8,128)(2,1)}), bf16[32,16,260]{2,1,0:T(8,128)(2,1)S(1)}, u32[]{:S(2)}, u32[]{:S(2)}) async-start(bf16[32,16,260]{2,1,0:T(8,128)(2,1)} %pad_maximum_fusion.1), calls=%async_computation.3 | async-start | bytes 786432 | tf_op jit(solution)/shard_map/all_to_all | solution.py:64
where the time goes:
time: 323 us; the launch traced here: 321 us
  blocking collectives  94.4 us (29%)
  matrix products  84.7 us (26%)
  other arithmetic  57.9 us (18%)
  local copies, waits for them, and re-layouts  41 us (13%)
  starting transfers between devices  26.7 us (8%)
  waiting for transfers between devices  15.8 us (5%)
    all_gather x1, blocking collectives, side_by_side(): whole = lax.all_gather(both, axis, axis=dim, tiled=True)  94.4 us
    reduce_sum x4, other arithmetic, per_block(): weight_sum = jnp.sum(weights, axis=1)  42.5 us
    dot_general x4, matrix products, per_block(): jnp.einsum('qd,kd->qk', query_block, key_head, preferred_element_type=jnp...  36 us
    dot_general x4, matrix products, per_block(): jnp.dot(weights.astype(jnp.bfloat16), value_head, preferred_element_type=...  28.4 us
    split x3, local copies, waits for them, and re-layouts, sent_together(): jnp.split(whole, [sum(widths[:k]) for k in range(1, len(widths))], axis=a...  18.5 us
    all_to_all x2, starting transfers between devices, copy_for_each(): return lax.all_to_all(copies, axis, split_axis=0, concat_axis=0, tiled=True)  17.1 us
    all_to_all x1, waiting for transfers between devices, sum_at_owner(): lax.all_to_all(cut_along(array, dim, peers), axis, 0, 0, tiled=True)  10.1 us
    dot_general x1, matrix products, per_device(): jnp.dot(normed, w_key, preferred_element_type=jnp.float32)  8.74 us
  transfers between devices with their start and end apart: 4, of which 2 were waited for; matrix products, arithmetic and copies ran while one was open for 14% of the time, Pallas kernels for 0%

commit v1 on v0

v1 whole, which is shorter than its diff:
```python
import functools

import jax
import jax.numpy as jnp
from jax import lax
from jax.experimental import pallas as pl
from jax.experimental.pallas import tpu as pltpu
from jax.sharding import PartitionSpec as P

HD = 64
BLOCK = 128
EPSILON = 1e-06
NEG_FILL = -1e30
FAR = 1 << 30
AXES = ("ctx", "head")
F32, BF16 = jnp.float32, jnp.bfloat16


def normed(rows):
    wide = rows.astype(F32)
    factor = lax.rsqrt(jnp.mean(wide * wide, axis=-1, keepdims=True) + EPSILON)
    return (wide * factor).astype(BF16)


def dot(a, b):
    return jnp.dot(a, b, preferred_element_type=F32)


def pick_dot(x, ones):
    first = x.astype(BF16)
    rest = x - first.astype(F32)
    second = rest.astype(BF16)
    third = (rest - second.astype(F32)).astype(BF16)
    ones = ones.astype(BF16)
    return dot(first, ones) + dot(second, ones) + dot(third, ones)


def iota(shape, dim):
    return lax.broadcasted_iota(jnp.int32, shape, dim)


def split_two(x):
    high = x.astype(BF16).astype(F32)
    return high, x - high


def latent_kernel(head_ref, lat_ref, wq_ref, wk_ref, wv_ref, q_ref, sv_ref, ss_ref):
    n = normed(lat_ref[...])
    q = (dot(n, wq_ref[...]) * HD ** (-0.5)).astype(BF16)
    k = dot(n, wk_ref[...]).astype(BF16)
    q_ref[...] = q
    sv_ref[...] = dot(n, wv_ref[...]).astype(BF16)
    prod = q.astype(F32) * k.astype(F32)
    width = prod.shape[1]
    heads = width // HD
    pick = (iota((width, 128), 0) // HD == iota((width, 128), 1) % heads).astype(F32)
    ss_ref[...] = pick_dot(prod, pick)


def latent_part(head, latents, w_query, w_key, w_value):
    rows, d = latents.shape
    width = w_query.shape[1]
    whole = lambda i, h: (0, 0)
    mine = lambda i, h: (0, h[0])
    return pl.pallas_call(
        latent_kernel,
        grid_spec=pltpu.PrefetchScalarGridSpec(
            num_scalar_prefetch=1,
            grid=(1,),
            in_specs=[
                pl.BlockSpec((rows, d), whole),
                pl.BlockSpec((d, width), whole),
                pl.BlockSpec((d, width), mine),
                pl.BlockSpec((d, width), mine),
            ],
            out_specs=[
                pl.BlockSpec((rows, width), whole),
                pl.BlockSpec((rows, width), whole),
                pl.BlockSpec((rows, 128), whole),
            ],
        ),
        out_shape=[
            jax.ShapeDtypeStruct((rows, width), BF16),
            jax.ShapeDtypeStruct((rows, width), BF16),
            jax.ShapeDtypeStruct((rows, 128), F32),
        ],
        name="latent_part",
        cost_estimate=pl.CostEstimate(flops=6 * rows * d * width, bytes_accessed=6 * d * width, transcendentals=0),
    )(head, latents, w_query, w_key, w_value)


def project_kernel(x_ref, wk_ref, wv_ref, k_ref, v_ref):
    n = normed(x_ref[...])
    k_ref[...] = dot(n, wk_ref[...]).astype(BF16)
    v_ref[...] = dot(n, wv_ref[...]).astype(BF16)


def project(prefix, w_key, w_value, tile=512):
    rows, d = prefix.shape
    cols = w_key.shape[1]
    by_row = lambda i: (i, 0)
    whole = lambda i: (0, 0)
    return pl.pallas_call(
        project_kernel,
        grid=(rows // tile,),
        in_specs=[
            pl.BlockSpec((tile, d), by_row),
            pl.BlockSpec((d, cols), whole),
            pl.BlockSpec((d, cols), whole),
        ],
        out_specs=[pl.BlockSpec((tile, cols), by_row)] * 2,
        out_shape=[jax.ShapeDtypeStruct((rows, cols), BF16)] * 2,
        name="project",
        compiler_params=pltpu.CompilerParams(vmem_limit_bytes=50 << 20),
        cost_estimate=pl.CostEstimate(flops=4 * rows * d * cols, bytes_accessed=6 * rows * d, transcendentals=0),
    )(prefix, w_key, w_value)


def attend_kernel(tile, q_ref, k_ref, v_ref, lpos_ref, kpos_ref, o_ref, bias, values):
    latents = bias.shape[0]
    step = pl.program_id(0)

    @pl.when(step == 0)
    def _():
        for t in range(latents // 128):
            at = pl.ds(t * 128, 128)
            own = jnp.transpose(jnp.broadcast_to(lpos_ref[:, at], (128, 128)))
            for c in range(kpos_ref.shape[1] // 128):
                cols = pl.ds(c * 128, 128)
                bias[at, cols] = jnp.where(kpos_ref[:, cols] < own, 0.0, NEG_FILL)

    values[:, :128] = v_ref[...]
    values[:, 128:] = jnp.ones((values.shape[0], 128), BF16)
    lane = iota((1, 128), 1)
    low = lane < HD
    first = step % 2 == 0
    lat_rows = q_ref.shape[2]
    per_tile = tile // lat_rows
    for t in range(latents // tile):
        own = pl.ds(t * per_tile, per_tile)
        q = q_ref[own, 0].reshape(tile, 128)
        sums, stats = [], jnp.zeros((tile, 128), F32)
        for j in range(2):
            qj = jnp.where(low == (j == 0), q, jnp.zeros_like(q))
            s = lax.dot_general(qj, k_ref[...], (((1,), (1,)), ((), ())), preferred_element_type=F32)
            s = s + bias[pl.ds(t * tile, tile), :]
            top = jnp.max(s, axis=1, keepdims=True)
            p = jnp.exp(s - top).astype(BF16)
            total = dot(p, values[...])
            sums.append(total[:, :128])
            t1, rest = split_two(top)
            t2, t3 = split_two(rest)
            s1, s2 = split_two(total[:, 128:])
            piece = jnp.where(
                lane < 4, t1, jnp.where(lane < 8, t2, jnp.where(lane < 12, t3, jnp.where(lane < 16, s1, s2)))
            )
            head = jnp.where(first, j, 2 + j)
            stats = jnp.where((lane % 4 == head) & (lane < 20), piece, stats)
        both = jnp.where(low, sums[0], sums[1]).astype(BF16).reshape(per_tile, lat_rows, 128)
        stats = stats.reshape(per_tile, lat_rows, 128)

        @pl.when(first)
        def _():
            o_ref[own, 0, :, 0:128] = both
            o_ref[own, 0, :, 256:384] = stats.astype(BF16)

        @pl.when(jnp.logical_not(first))
        def _():
            o_ref[own, 0, :, 128:256] = both
            o_ref[own, 0, :, 256:384] = (o_ref[own, 0, :, 256:384].astype(F32) + stats).astype(BF16)


def attend(queries, keys, values, lpos, kpos, tile=128):
    ctx, groups, lat_rows, width = queries.shape
    latents, rows = ctx * lat_rows, keys.shape[0]
    pairs = groups * width // 128
    per = width // 128
    return pl.pallas_call(
        functools.partial(attend_kernel, tile),
        grid=(pairs,),
        in_specs=[
            pl.BlockSpec((ctx, 1, lat_rows, 128), lambda i: (0, i // per, 0, i % per)),
            pl.BlockSpec((rows, 128), lambda i: (0, i)),
            pl.BlockSpec((rows, 128), lambda i: (0, i)),
            pl.BlockSpec((1, latents), lambda i: (0, 0)),
            pl.BlockSpec((1, rows), lambda i: (0, 0)),
        ],
        out_specs=pl.BlockSpec((ctx, 1, lat_rows, width + 128), lambda i: (0, i // per, 0, 0)),
        out_shape=jax.ShapeDtypeStruct((ctx, groups, lat_rows, width + 128), BF16),
        scratch_shapes=[pltpu.VMEM((latents, rows), F32), pltpu.VMEM((rows, 256), BF16)],
        name="attend",
        compiler_params=pltpu.CompilerParams(vmem_limit_bytes=56 << 20),
        cost_estimate=pl.CostEstimate(
            flops=4 * latents * rows * width * groups,
            bytes_accessed=4 * rows * width * groups,
            transcendentals=latents * rows * 2 * pairs,
        ),
    )(queries, keys, values, lpos, kpos)


def combine_kernel(parts_ref, ss_ref, sv_ref, out_ref):
    shards, rows, wide = parts_ref.shape
    parts = parts_ref[...]
    stats = parts[:, :, 256:].reshape(shards * rows, 128)
    r, c = iota((128, 128), 0), iota((128, 128), 1)
    join = ((r < 12) & (r % 4 == c % 4)).astype(BF16)
    tops = dot(stats, join).reshape(shards, rows, 128)
    own = ss_ref[...]
    top = jnp.maximum(jnp.max(tops, axis=0), own)
    scale = jnp.exp(tops - top[None]).reshape(shards * rows, 128)
    high, rest = split_two(scale)
    lane = iota((1, 128), 1)
    pieces = jnp.where(lane < 4, high, jnp.where(lane < 8, rest, 0.0)).astype(BF16)
    r, c = iota((128, wide), 0), iota((128, wide), 1)
    head = jnp.where(c < 256, c // HD, jnp.where((c >= 268) & (c < 276), c % 4, 4))
    spread = ((r < 8) & (r % 4 == head)).astype(BF16)
    scales = dot(pieces, spread).reshape(shards, rows, wide)
    total = jnp.sum(scales * parts.astype(F32), axis=0)
    r, c = iota((128, 256), 0), iota((128, 256), 1)
    denominator = pick_dot(total[:, 256:], ((r >= 12) & (r < 20) & (r % 4 == c // HD)).astype(F32))
    self_weight = pick_dot(jnp.exp(own - top), ((r < 4) & (r == c // HD)).astype(F32))
    numerator = total[:, :256] + self_weight * sv_ref[...].astype(F32)
    out_ref[...] = (numerator / (denominator + self_weight)).astype(BF16)


def combine(parts, self_score, self_value):
    return pl.pallas_call(
        combine_kernel,
        out_shape=jax.ShapeDtypeStruct(self_value.shape, BF16),
        name="combine",
        compiler_params=pltpu.CompilerParams(vmem_limit_bytes=40 << 20),
    )(parts, self_score, self_value)


def per_device(prefix, keep_blocks, keep_count, latent_inputs, latent_pos, w_query, w_key, w_value):
    ctx_size, head_size = lax.axis_size("ctx"), lax.axis_size("head")
    shard = lax.axis_index("ctx") * head_size + lax.axis_index("head")
    rows = prefix.shape[0]
    blocks = rows // BLOCK
    order = jnp.arange(blocks, dtype=jnp.int32)
    match = (keep_blocks.reshape(1, blocks) == order[:, None]) & (order[None, :] < keep_count.reshape(1, 1))
    kept = jnp.repeat(jnp.any(match, axis=1), BLOCK)
    kpos = jnp.where(kept, shard * rows + jnp.arange(rows, dtype=jnp.int32), FAR)[None, :]

    head = lax.axis_index("head").astype(jnp.int32).reshape(1)
    query, self_value, self_score = latent_part(head, latent_inputs, w_query, w_key, w_value)
    lat_rows, width = query.shape
    queries = lax.all_gather(query, AXES, axis=0).reshape(ctx_size, head_size, lat_rows, width)
    keys, values = project(prefix, w_key, w_value)
    parts = attend(queries, keys, values, latent_pos.reshape(1, -1), kpos)
    parts = parts.reshape(ctx_size * head_size, lat_rows, width + 128)
    parts = lax.all_to_all(parts, AXES, 0, 0, tiled=True)
    return combine(parts, self_score, self_value)


def solution(mesh):
    return jax.shard_map(
        per_device,
        mesh=mesh,
        in_specs=(
            P(("ctx", "head"), None),
            P("head", "ctx", None),
            P("head", "ctx"),
            P("ctx", None),
            P(),
            P(None, "head"),
            P(),
            P(),
        ),
        out_specs=P("ctx", "head"),
        check_vma=False,
    )
```

time: 323 us -> 160 us (0.50)
  matrix products: 84.7 us -> 0 us
  blocking collectives: 94.4 us -> 30.3 us
  Pallas kernels: 0 us -> 60.7 us
  other arithmetic: 57.9 us -> 0.73 us
  local copies, waits for them, and re-layouts: 41 us -> 0.09 us
  waiting for transfers between devices: 15.8 us -> 53.7 us
  starting transfers between devices: 26.7 us -> 0.01 us
  between operations: 0.87 us -> 14.1 us
    all_gather x1 -> x0, blocking collectives: 94.4 us -> none  [side_by_side(): whole = lax.all_gather(both, axis, axis=dim, tiled=True)]
    dot_general x13 -> x0, matrix products: 84.7 us -> none  [the longest x4 36 us: per_block(): jnp.einsum('qd,kd->qk', query_block, key_head, preferred_element_type=jnp...]
    pallas_call x0 -> x4, Pallas kernels: none -> 60.7 us  [the longest x1 43.1 us: attend(): pl.pallas_call(functools.partial(attend_kernel, tile), grid=(pairs,), in_...]
    all_gather x0 -> x1, waiting for transfers between devices: none -> 53.7 us  [per_device(): lax.all_gather(query, AXES, axis=0)]
    reduce_sum x8 -> x0, other arithmetic: 46.9 us -> none  [the longest x4 42.5 us: per_block(): weight_sum = jnp.sum(weights, axis=1)]
    all_to_all x0 -> x1, blocking collectives: none -> 30.3 us  [per_device(): parts = lax.all_to_all(parts, AXES, 0, 0, tiled=True)]
    all_to_all x4 -> x0, starting transfers between devices: 26.7 us -> none  [the longest x2 17.1 us: copy_for_each(): return lax.all_to_all(copies, axis, split_axis=0, concat_axis=0, tiled=True)]
    split x4 -> x0, local copies, waits for them, and re-layouts: 18.7 us -> none  [the longest x3 18.5 us: sent_together(): jnp.split(whole, [sum(widths[:k]) for k in range(1, len(widths))], axis=a...]
  transfers between devices with their start and end apart: 4 -> 1, of which waited for: 2 -> 1; matrix products, arithmetic and copies ran while one was open for 14% -> 1% of each run, Pallas kernels for 0% -> 8%
where the time goes in v1:
time: 160 us
  Pallas kernels  60.7 us (38%)
  waiting for transfers between devices  53.7 us (34%)
  blocking collectives  30.3 us (19%)
  between operations  14.1 us (9%)
    all_gather x1, waiting for transfers between devices, per_device(): lax.all_gather(query, AXES, axis=0)  53.7 us
    pallas_call x1, Pallas kernels, attend(): pl.pallas_call(functools.partial(attend_kernel, tile), grid=(pairs,), in_...  43.1 us
    all_to_all x1, blocking collectives, per_device(): parts = lax.all_to_all(parts, AXES, 0, 0, tiled=True)  30.3 us
    pallas_call x1, Pallas kernels, project(): pl.pallas_call(project_kernel, grid=(rows // tile,), in_specs=[pl.BlockSp...  13 us
  transfers between devices with their start and end apart: 1, of which 1 were waited for; matrix products, arithmetic and copies ran while one was open for 1% of the time, Pallas kernels for 8%

profile of v1, /device:TPU:1, one launch (start us, length us, event | category | flops | bytes accessed | tf_op | source)
XLA Modules:
  0.0 159.6 jit_solution(17055391188949377806)
XLA Ops:
  6.5 0.0 all-gather.3.cloned.1.call-start
  6.5 0.0 copy-start.3
  6.5 0.0 copy-start
  6.5 2.6 %latent_part.1 = (bf16[16,256]{1,0:T(8,128)(2,1)}, bf16[16,256]{1,0:T(8,128)(2,1)}, f32[16,128]{1,0:T(8,128)}) custom-call(s32[1]{0:T(128)} %bitcast.head_ref, bf16[16,1024]{1,0:T(8,128)(2,1)} %lat_ref.1, bf16[1024,256]{1,0:T(8,128)(2,1)} %wq_ref.1, bf16[1024,1024]{1,0:T(8,128)(2,1)} %wk_ref.3, bf16[1024,1024]{1,0:T(8,128)(2,1)} %wv_ref.3), custom_call_target="tpu_custom_call" | custom-call | flops 25165824 | bytes 1572864 | tf_op jit(solution)/shard_map/latent_part/pallas_call | solution.py:65
  9.2 0.0 all-gather.3.cloned.1.call-update
  9.9 0.0 copy-done.3
  9.9 0.1 fusion.1
  10.0 0.1 broadcast_bitcast_fusion
  10.1 0.6 bitcast_select_fusion.kpos_ref
  10.7 0.0 copy-done
  10.7 13.0 %project.1 = (bf16[2048,1024]{1,0:T(8,128)(2,1)}, bf16[2048,1024]{1,0:T(8,128)(2,1)}) custom-call(bf16[2048,1024]{1,0:T(8,128)(2,1)} %x_ref.1, bf16[1024,1024]{1,0:T(8,128)(2,1)S(1)} %copy-done, bf16[1024,1024]{1,0:T(8,128)(2,1)} %wv_ref.3), custom_call_target="tpu_custom_call" | custom-call | flops 8589934592 | bytes 12582912 | tf_op jit(solution)/shard_map/project/pallas_call | solution.py:103
  23.7 53.7 %all-gather.3.cloned.1.call-done = bf16[2048,256]{1,0:T(8,128)(2,1)} async-done(((bf16[16,256]{1,0:T(8,128)(2,1)}), bf16[2048,256]{1,0:T(8,128)(2,1)}) %all-gather.3.cloned.1.call-update) | async-done | bytes 1048592 | tf_op jit(solution)/shard_map/all_gather | solution.py:248
  77.4 43.1 %attend.1 = bf16[32,4,16,384]{3,2,1,0:T(8,128)(2,1)} custom-call(bf16[32,4,16,256]{3,2,1,0:T(8,128)(2,1)} %bitcast.13, bf16[2048,1024]{1,0:T(8,128)(2,1)} %get-tuple-element.11.k_ref, bf16[2048,1024]{1,0:T(8,128)(2,1)} %get-tuple-element.12.v_ref, s32[1,512]{1,0:T(1,128)} %bitcast.14, s32[1,2048]{1,0:T(1,128)} %bitcast_select_fusion.kpos_ref), custom_call_target="tpu_custom_call" | custom-call | flops 4294967296 | bytes 8388608 | tf_op jit(solution)/shard_map/attend/pallas_call | solution.py:178
  120.5 0.0 copy-start.1
  120.5 0.0 copy-start.2
  120.5 30.3 %all_to_all.5.parts_ref = bf16[128,16,384]{2,1,0:T(8,128)(2,1)S(1)} all-to-all(bf16[128,16,384]{2,1,0:T(8,128)(2,1)} %bitcast.12), channel_id=1, replica_groups=mesh['ctx'=32,'head'=4] {'ctx','head'}, dimensions={0} | all-to-all | bytes 3145728 | tf_op jit(solution)/shard_map/all_to_all | solution.py:252
  150.8 0.0 copy-done.1
  150.8 0.0 copy-done.2
  150.8 2.0 %combine.1 = bf16[16,256]{1,0:T(8,128)(2,1)} custom-call(bf16[128,16,384]{2,1,0:T(8,128)(2,1)S(1)} %all_to_all.5.parts_ref, f32[16,128]{1,0:T(8,128)S(1)} %copy-done.2, bf16[16,256]{1,0:T(8,128)(2,1)S(1)} %copy-done.1), custom_call_target="tpu_custom_call" | custom-call | tf_op jit(solution)/shard_map/combine/pallas_call | solution.py:227
  (1 shorter events, 0.0 us)
Async XLA Ops:
  6.5 70.8 %all-gather.3.cloned.1.call-start = ((), (), s32[]{:S(2)}) async-start(), calls=%async_computation.1 | async-start | bytes 1056768 | tf_op jit(solution)/shard_map/all_gather | solution.py:248
  6.5 3.3 %copy-start.3 = (s32[1,1,16]{2,1,0:T(1,128)S(1)}, s32[1,1,16]{2,1,0:T(1,128)}, u32[]{:S(2)}) copy-start(s32[1,1,16]{2,1,0:T(1,128)} %param.9) | copy-start | bytes 196
  6.5 4.1 %copy-start = (bf16[1024,1024]{1,0:T(8,128)(2,1)S(1)}, bf16[1024,1024]{1,0:T(8,128)(2,1)}, u32[]{:S(2)}) copy-start(bf16[1024,1024]{1,0:T(8,128)(2,1)} %wk_ref.3) | copy-start | bytes 6291460
  120.5 30.3 %copy-start.1 = (bf16[16,256]{1,0:T(8,128)(2,1)S(1)}, bf16[16,256]{1,0:T(8,128)(2,1)}, u32[]{:S(2)}) copy-start(bf16[16,256]{1,0:T(8,128)(2,1)} %get-tuple-element.14.sv_ref) | copy-start | bytes 24580
  120.5 30.3 %copy-start.2 = (f32[16,128]{1,0:T(8,128)S(1)}, f32[16,128]{1,0:T(8,128)}, u32[]{:S(2)}) copy-start(f32[16,128]{1,0:T(8,128)} %get-tuple-element.13.ss_ref) | copy-start | bytes 24580
Sparse Core Ops, SparseCore 0:
  10.1 67.1 all-gather.2

commit v2 on v1

v2 whole, which is shorter than its diff:
```python
import functools

import jax
import jax.numpy as jnp
from jax import lax
from jax.experimental import pallas as pl
from jax.experimental.pallas import tpu as pltpu
from jax.sharding import PartitionSpec as P

HD = 64
BLOCK = 128
EPSILON = 1e-06
NEG_FILL = -1e30
FAR = 1 << 30
MESH = pl.DeviceIdType.MESH
F32, BF16 = jnp.float32, jnp.bfloat16


def normed(rows):
    wide = rows.astype(F32)
    factor = lax.rsqrt(jnp.mean(wide * wide, axis=-1, keepdims=True) + EPSILON)
    return (wide * factor).astype(BF16)


def dot(a, b):
    return jnp.dot(a, b, preferred_element_type=F32)


def pick_dot(x, ones):
    first = x.astype(BF16)
    rest = x - first.astype(F32)
    second = rest.astype(BF16)
    third = (rest - second.astype(F32)).astype(BF16)
    ones = ones.astype(BF16)
    return dot(first, ones) + dot(second, ones) + dot(third, ones)


def iota(shape, dim):
    return lax.broadcasted_iota(jnp.int32, shape, dim)


def split_two(x):
    high = x.astype(BF16).astype(F32)
    return high, x - high


def combine(parts_ref, own, self_value):
    shards, rows, wide = parts_ref.shape
    parts = parts_ref[...]
    stats = parts[:, :, 256:].reshape(shards * rows, 128)
    r, c = iota((128, 128), 0), iota((128, 128), 1)
    join = ((r < 12) & (r % 4 == c % 4)).astype(BF16)
    tops = dot(stats, join).reshape(shards, rows, 128)
    top = jnp.maximum(jnp.max(tops, axis=0), own)
    scale = jnp.exp(tops - top[None]).reshape(shards * rows, 128)
    high, rest = split_two(scale)
    lane = iota((1, 128), 1)
    pieces = jnp.where(lane < 4, high, jnp.where(lane < 8, rest, 0.0)).astype(BF16)
    r, c = iota((128, wide), 0), iota((128, wide), 1)
    head = jnp.where(c < 256, c // HD, jnp.where((c >= 268) & (c < 276), c % 4, 4))
    spread = ((r < 8) & (r % 4 == head)).astype(BF16)
    scales = dot(pieces, spread).reshape(shards, rows, wide)
    total = jnp.sum(scales * parts.astype(F32), axis=0)
    r, c = iota((128, 256), 0), iota((128, 256), 1)
    denominator = pick_dot(total[:, 256:], ((r >= 12) & (r < 20) & (r % 4 == c // HD)).astype(F32))
    self_weight = pick_dot(jnp.exp(own - top), ((r < 4) & (r == c // HD)).astype(F32))
    numerator = total[:, :256] + self_weight * self_value
    return (numerator / (denominator + self_weight)).astype(BF16)


def totals_of(lane, head, top, weight_sum):
    t1, rest = split_two(top)
    t2, t3 = split_two(rest)
    s1, s2 = split_two(weight_sum)
    piece = jnp.where(lane < 4, t1, jnp.where(lane < 8, t2, jnp.where(lane < 12, t3, jnp.where(lane < 16, s1, s2))))
    return jnp.where((lane % 4 == head) & (lane < 20), piece, 0.0)


def whole_kernel(
    sizes, lat_ref, wq_ref, lpos_ref, kpos_ref, x_hbm, wk_hbm, wv_hbm, out_ref,
    x, wk, wv, keys, values, queries, bias, scores, weights, parts, arrived,
    x_sem, w_sem, q_send, q_recv, p_send, p_recv,
):
    ctx_size, head_size = sizes
    shards = ctx_size * head_size
    me_c, me_h = lax.axis_index("ctx"), lax.axis_index("head")
    me = me_c * head_size + me_h
    rows = x.shape[0]
    tile = 512
    copies = [pltpu.make_async_copy(wk_hbm, wk, w_sem.at[0]), pltpu.make_async_copy(wv_hbm, wv, w_sem.at[1])]
    copies[0].start()

    def x_copy(t):
        at = pl.ds(pl.multiple_of(t * tile, tile), tile)
        return pltpu.make_async_copy(x_hbm.at[at], x.at[at], x_sem.at[t])

    x_copy(0).start()
    copies[1].start()
    for t in range(1, rows // tile):
        x_copy(t).start()

    barrier = pltpu.get_barrier_semaphore()

    def peer(i):
        other = lax.rem(me + i, shards)
        return (lax.div(other, head_size), lax.rem(other, head_size))

    def greet(i, carry):
        pl.semaphore_signal(barrier, inc=1, device_id=peer(i), device_id_type=MESH)
        return carry

    lax.fori_loop(1, shards, greet, 0)

    lat_n = normed(lat_ref[...])
    query = (dot(lat_n, wq_ref[...]) * HD ** (-0.5)).astype(BF16)
    queries[me_h * ctx_size + me_c] = query
    pl.semaphore_wait(barrier, shards - 1)

    def send_query(i, carry):
        mine = queries.at[me_h * ctx_size + me_c]
        pltpu.make_async_remote_copy(
            src_ref=mine, dst_ref=mine, send_sem=q_send, recv_sem=q_recv, device_id=peer(i), device_id_type=MESH
        ).start()
        return carry

    lax.fori_loop(1, shards, send_query, 0)

    lane = iota((1, 128), 1)
    low = lane < HD
    latents, lat_rows = bias.shape[0], lat_ref.shape[0]
    for t in range(latents // 128):
        at = pl.ds(t * 128, 128)
        own = jnp.transpose(jnp.broadcast_to(lpos_ref[:, at], (128, 128)))
        for c in range(rows // 128):
            cols = pl.ds(c * 128, 128)
            bias[at, cols] = jnp.where(kpos_ref[:, cols] < own, 0.0, NEG_FILL)
    values[:, :, 128:] = jnp.ones(values.shape[:2] + (128,), BF16)

    copies[0].wait()
    copies[1].wait()
    pairs = keys.shape[0]

    def project(t, carry):
        x_copy(t).wait()
        at = pl.ds(pl.multiple_of(t * tile, tile), tile)
        n = normed(x[at, :])
        k = dot(n, wk[...]).astype(BF16)
        for p in range(pairs):
            keys[p, at, :] = k[:, p * 128:(p + 1) * 128]
        v = dot(n, wv[...]).astype(BF16)
        for p in range(pairs):
            values[p, at, 0:128] = v[:, p * 128:(p + 1) * 128]
        return carry

    lax.fori_loop(0, rows // tile, project, 0)

    width = wq_ref.shape[1]
    mine = pl.ds(pl.multiple_of(me_h * width, width), width)
    self_key = dot(lat_n, wk[:, mine]).astype(BF16)
    self_value = dot(lat_n, wv[:, mine]).astype(BF16).astype(F32)
    prod = query.astype(F32) * self_key.astype(F32)
    self_score = pick_dot(prod, iota((width, 128), 0) // HD == iota((width, 128), 1) % (width // HD))

    count = pl.ds(0, shards - 1)
    landed = queries.at[count]
    pltpu.make_async_copy(landed, landed, q_recv).wait()
    pltpu.make_async_copy(landed, landed, q_send).wait()

    step_rows = 128
    per = step_rows // lat_rows
    units = [(t, j) for t in range(latents // step_rows) for j in range(2)]
    chunk, part_rows = 256, 1024

    def group(step, carry):
        g = lax.rem(me_h + 1 + step, head_size)
        top = None
        stats = None
        for u in range(-1, len(units)):
            q = peak = total = None
            nxt = u + 1
            if nxt < len(units):
                t, j = units[nxt]
                q = queries[pl.ds(g * ctx_size + t * per, per), :, j * 128:(j + 1) * 128].reshape(step_rows, 128)
                zero = jnp.zeros_like(q)
                q = jnp.concatenate([jnp.where(low, q, zero), jnp.where(low, zero, q)], 0)
            for c in range(rows // chunk):
                at = pl.ds(c * chunk, chunk)
                if nxt < len(units):
                    t, j = units[nxt]
                    s = lax.dot_general(
                        q, keys[g * 2 + j, at, :], (((1,), (1,)), ((), ())), preferred_element_type=F32
                    )
                    off = bias[pl.ds(t * step_rows, step_rows), at]
                    s = jnp.concatenate([s[:step_rows] + off, s[step_rows:] + off], 0)
                    scores[nxt % 2, :, at] = s
                    for i in range(chunk // 128):
                        piece = s[:, i * 128:(i + 1) * 128]
                        peak = piece if peak is None else jnp.maximum(peak, piece)
                if u >= 0:
                    t, j = units[u]
                    weights[:, at] = jnp.exp(scores[u % 2, :, at] - top).astype(BF16)
                    if (c + 1) * chunk % part_rows == 0:
                        at = pl.ds((c + 1) * chunk - part_rows, part_rows)
                        more = dot(weights[:, at], values[g * 2 + j, at, :])
                        total = more if total is None else total + more
            if u >= 0:
                t, j = units[u]
                own = pl.ds(t * per, per)
                both = jnp.where(low, total[:step_rows, :128], total[step_rows:, :128]).astype(BF16)
                parts[g, own, :, j * 128:(j + 1) * 128] = both.reshape(per, lat_rows, 128)
                new = totals_of(lane, 2 * j, top[:step_rows], total[:step_rows, 128:])
                new = new + totals_of(lane, 2 * j + 1, top[step_rows:], total[step_rows:, 128:])
                if j == 0:
                    stats = new
                else:
                    parts[g, own, :, 256:384] = (stats + new).astype(BF16).reshape(per, lat_rows, 128)
            if peak is not None:
                top = jnp.max(peak, axis=1, keepdims=True)

        def send_part(i, carry):
            c = lax.rem(me_c + i, ctx_size)
            pltpu.make_async_remote_copy(
                src_ref=parts.at[g, c], dst_ref=arrived.at[me], send_sem=p_send, recv_sem=p_recv,
                device_id=(c, g), device_id_type=MESH,
            ).start()
            return carry

        lax.fori_loop(lax.div(step + 1, head_size), ctx_size, send_part, 0)
        return carry

    lax.fori_loop(0, head_size, group, 0)
    arrived[me] = parts[me_h, me_c]
    landed = arrived.at[count]
    pltpu.make_async_copy(landed, landed, p_recv).wait()
    out_ref[...] = combine(arrived, self_score, self_value)
    pltpu.make_async_copy(landed, landed, p_send).wait()


def per_device(prefix, keep_blocks, keep_count, latent_inputs, latent_pos, w_query, w_key, w_value):
    ctx_size, head_size = lax.axis_size("ctx"), lax.axis_size("head")
    shard = lax.axis_index("ctx") * head_size + lax.axis_index("head")
    rows, d = prefix.shape
    blocks = rows // BLOCK
    order = jnp.arange(blocks, dtype=jnp.int32)
    match = (keep_blocks.reshape(1, blocks) == order[:, None]) & (order[None, :] < keep_count.reshape(1, 1))
    kept = jnp.repeat(jnp.any(match, axis=1), BLOCK)
    kpos = jnp.where(kept, shard * rows + jnp.arange(rows, dtype=jnp.int32), FAR)[None, :]
    lat_rows, width = latent_inputs.shape[0], w_query.shape[1]
    latents, cols = lat_rows * ctx_size, width * head_size
    pairs = cols // 128
    vmem = pl.BlockSpec(memory_space=pltpu.VMEM)
    hbm = pl.BlockSpec(memory_space=pl.ANY)
    dma = pltpu.SemaphoreType.DMA
    return pl.pallas_call(
        functools.partial(whole_kernel, (ctx_size, head_size)),
        in_specs=[vmem] * 4 + [hbm] * 3,
        out_specs=vmem,
        out_shape=jax.ShapeDtypeStruct((lat_rows, width), BF16),
        scratch_shapes=[
            pltpu.VMEM((rows, d), BF16),
            pltpu.VMEM((d, cols), BF16),
            pltpu.VMEM((d, cols), BF16),
            pltpu.VMEM((pairs, rows, 128), BF16),
            pltpu.VMEM((pairs, rows, 256), BF16),
            pltpu.VMEM((head_size * ctx_size, lat_rows, width), BF16),
            pltpu.VMEM((latents, rows), F32),
            pltpu.VMEM((2, 256, rows), F32),
            pltpu.VMEM((256, rows), BF16),
            pltpu.VMEM((head_size, ctx_size, lat_rows, width + 128), BF16),
            pltpu.VMEM((ctx_size * head_size, lat_rows, width + 128), BF16),
            dma((rows // 512,)),
            dma((2,)),
            dma,
            dma,
            dma,
            dma,
        ],
        name="whole",
        compiler_params=pltpu.CompilerParams(
            collective_id=0, has_side_effects=True, vmem_limit_bytes=60 << 20
        ),
        cost_estimate=pl.CostEstimate(
            flops=4 * rows * d * cols + 4 * latents * rows * cols,
            bytes_accessed=2 * rows * d + 4 * d * cols,
            transcendentals=latents * rows * 2 * pairs,
        ),
    )(latent_inputs, w_query, latent_pos.reshape(1, -1), kpos, prefix, w_key, w_value)


def solution(mesh):
    return jax.shard_map(
        per_device,
        mesh=mesh,
        in_specs=(
            P(("ctx", "head"), None),
            P("head", "ctx", None),
            P("head", "ctx"),
            P("ctx", None),
            P(),
            P(None, "head"),
            P(),
            P(),
        ),
        out_specs=P("ctx", "head"),
        check_vma=False,
    )
```

time: 160 us -> 66.3 us (0.41)
  waiting for transfers between devices: 53.7 us -> 0 us
  blocking collectives: 30.3 us -> 0 us
  between operations: 14.1 us -> 0.67 us
  Pallas kernels: 60.7 us -> 62.7 us
    all_gather x1 -> x0, waiting for transfers between devices: 53.7 us -> none  [per_device(): lax.all_gather(query, AXES, axis=0)]
    all_to_all x1 -> x0, blocking collectives: 30.3 us -> none  [per_device(): parts = lax.all_to_all(parts, AXES, 0, 0, tiled=True)]
    pallas_call x4 -> x1, Pallas kernels: 60.7 us -> 62.7 us  [per_device(): pl.pallas_call(functools.partial(whole_kernel, (ctx_size, head_size)), in...]
  transfers between devices with their start and end apart: 1 -> 0, of which waited for: 1 -> 0; matrix products, arithmetic and copies ran while one was open for 1% -> 0% of each run, Pallas kernels for 8% -> 0%
where the time goes in v2:
time: 66.3 us; the launch traced here: 66.2 us
  Pallas kernels  62.7 us (95%)
  other arithmetic  1.4 us (2%)
  local copies, waits for them, and re-layouts  1.37 us (2%)
  between operations  0.67 us (1%)
    pallas_call x1, Pallas kernels, per_device(): pl.pallas_call(functools.partial(whole_kernel, (ctx_size, head_size)), in...  62.7 us
    unnamed x2, local copies, waits for them, and re-layouts  1.37 us

profile of v2, /device:TPU:1, one launch (start us, length us, event | category | flops | bytes accessed | tf_op | source)
XLA Modules:
  0.0 66.2 jit_solution(3046125639126369826)
XLA Ops:
  0.7 0.8 %fusion.1 = pred[16]{0:T(512)(128)(4,1)S(1)} fusion(s32[16]{0:T(128)} %bitcast.10, pred[16]{0:T(512)(128)(4,1)S(1)} %iota_compare_fusion.1), kind=kLoop, calls=%fused_computation.3 | loop fusion | flops 752 | bytes 96 | tf_op jit(solution)/shard_map/reduce_or | solution.py:246
  1.4 0.1 broadcast_bitcast_fusion
  1.5 0.6 bitcast_select_fusion.kpos_ref
  2.1 62.7 %whole.1 = bf16[16,256]{1,0:T(8,128)(2,1)} custom-call(bf16[16,1024]{1,0:T(8,128)(2,1)} %lat_ref.1, bf16[1024,256]{1,0:T(8,128)(2,1)} %wq_ref.1, s32[1,512]{1,0:T(1,128)} %bitcast.9, s32[1,2048]{1,0:T(1,128)} %bitcast_select_fusion.kpos_ref, bf16[2048,1024]{1,0:T(8,128)(2,1)} %x_hbm.1, bf16[1024,1024]{1,0:T(8,128)(2,1)} %wk_hbm.1, bf16[1024,1024]{1,0:T(8,128)(2,1)} %wv_hbm.1), custom_call_target="tpu_custom_call" | custom-call | flops 12884901888 | bytes 8388608 | tf_op jit(solution)/shard_map/whole/pallas_call | solution.py:254
  64.9 1.3 %copy.13 = bf16[16,256]{1,0:T(8,128)(2,1)} copy(bf16[16,256]{1,0:T(8,128)(2,1)} %whole.1) | data formatting | bytes 16384
  (1 shorter events, 0.0 us)

commit v3 on v2

v3 whole, which is shorter than its diff:
```python
import functools

import jax
import jax.numpy as jnp
from jax import lax
from jax.experimental import pallas as pl
from jax.experimental.pallas import tpu as pltpu
from jax.sharding import PartitionSpec as P

HD = 64
BLOCK = 128
EPSILON = 1e-06
NEG_FILL = -1e30
FAR = 1 << 30
MESH = pl.DeviceIdType.MESH
F32, BF16 = jnp.float32, jnp.bfloat16


def normed(rows):
    wide = rows.astype(F32)
    factor = lax.rsqrt(jnp.mean(wide * wide, axis=-1, keepdims=True) + EPSILON)
    return (wide * factor).astype(BF16)


def dot(a, b):
    return jnp.dot(a, b, preferred_element_type=F32)


def pick_dot(x, ones):
    first = x.astype(BF16)
    rest = x - first.astype(F32)
    second = rest.astype(BF16)
    third = (rest - second.astype(F32)).astype(BF16)
    ones = ones.astype(BF16)
    return dot(first, ones) + dot(second, ones) + dot(third, ones)


def iota(shape, dim):
    return lax.broadcasted_iota(jnp.int32, shape, dim)


def split_two(x):
    high = x.astype(BF16).astype(F32)
    return high, x - high


def spread_scale(scale, wide):
    high, rest = split_two(scale)
    lane = iota((1, 128), 1)
    pieces = jnp.where(lane < 4, high, jnp.where(lane < 8, rest, 0.0)).astype(BF16)
    r, c = iota((128, wide), 0), iota((128, wide), 1)
    head = jnp.where(c < 256, c // HD, jnp.where((c >= 268) & (c < 276), c % 4, 4))
    return dot(pieces, ((r < 8) & (r % 4 == head)).astype(BF16))


def combine(parts_ref, own, self_value):
    shards, rows, wide = parts_ref.shape
    parts = parts_ref[...]
    stats = parts[:, :, 256:].reshape(shards * rows, 128)
    r, c = iota((128, 128), 0), iota((128, 128), 1)
    join = ((r < 12) & (r % 4 == c % 4)).astype(BF16)
    tops = dot(stats, join).reshape(shards, rows, 128)
    top = jnp.maximum(jnp.max(tops, axis=0), own)
    scale = jnp.exp(tops - top[None]).reshape(shards * rows, 128)
    scales = spread_scale(scale, wide).reshape(shards, rows, wide)
    total = jnp.sum(scales * parts.astype(F32), axis=0)
    r, c = iota((128, 256), 0), iota((128, 256), 1)
    denominator = pick_dot(total[:, 256:], ((r >= 12) & (r < 20) & (r % 4 == c // HD)).astype(F32))
    self_weight = pick_dot(jnp.exp(own - top), ((r < 4) & (r == c // HD)).astype(F32))
    numerator = total[:, :256] + self_weight * self_value
    return (numerator / (denominator + self_weight)).astype(BF16)


def pieces_of(lane, top, weight_sum):
    t1, rest = split_two(top)
    t2, t3 = split_two(rest)
    s1, s2 = split_two(weight_sum)
    piece = jnp.where(lane < 4, t1, jnp.where(lane < 8, t2, jnp.where(lane < 12, t3, jnp.where(lane < 16, s1, s2))))
    return jnp.where(lane < 20, piece, 0.0)


def totals_of(lane, head, top, weight_sum):
    return jnp.where(lane % 4 == head, pieces_of(lane, top, weight_sum), 0.0)


def merge(mine, theirs):
    rows, wide = mine.shape
    both = jnp.concatenate([mine, theirs], 0)
    r, c = iota((128, 128), 0), iota((128, 128), 1)
    tops = dot(both[:, 256:], ((r < 12) & (r % 4 == c % 4)).astype(BF16))
    top = jnp.maximum(tops[:rows], tops[rows:])
    scaled = both.astype(F32) * spread_scale(jnp.exp(tops - jnp.concatenate([top, top], 0)), wide)
    total = scaled[:rows] + scaled[rows:]
    weight_sum = pick_dot(total[:, 256:], (r >= 12) & (r < 20) & (r % 4 == c % 4))
    return total[:, :256], pieces_of(iota((1, 128), 1), top, weight_sum)


def whole_kernel(
    sizes, lat_ref, wq_ref, lpos_ref, kb_ref, kc_ref, x_hbm, wk_hbm, wv_hbm, out_ref,
    x, wk, wv, keys, values, own_query, queries, bias, scores, weights, tops, own, other, merged, arrived,
    x_sem, w_sem, q_send, q_recv, f_send, f_recv, o_send, o_recv, p_send, p_recv,
):
    ctx_size, planes = sizes
    chips = ctx_size // 2
    near = chips // 2
    me_c, me_h = lax.axis_index("ctx"), lax.axis_index("head")
    me_p, me_k = lax.div(me_c, 2), lax.rem(me_c, 2)
    me_half = lax.div(me_p, near)
    sibling = (me_p * 2 + 1 - me_k, me_h)
    rows = x.shape[0]
    tile = 512

    def x_copy(t):
        at = pl.ds(pl.multiple_of(t * tile, tile), tile)
        return pltpu.make_async_copy(x_hbm.at[at], x.at[at], x_sem.at[t])

    wk_copy = pltpu.make_async_copy(wk_hbm, wk, w_sem.at[0])
    wv_copy = pltpu.make_async_copy(wv_hbm, wv, w_sem.at[1])
    wk_copy.start()
    x_copy(0).start()
    wv_copy.start()
    for t in range(1, rows // tile):
        x_copy(t).start()

    barrier = pltpu.get_barrier_semaphore()

    def peer(i):
        away = 1 + lax.div(i, chips)
        plane = lax.rem(jnp.where(me_half == 0, me_h + planes - away, me_h + away), planes)
        chip = lax.rem(me_p + lax.rem(i, chips), chips)
        return (chip * 2 + me_k, plane)

    def greet(i, carry):
        pl.semaphore_signal(barrier, inc=1, device_id=peer(i), device_id_type=MESH)
        return carry

    own_place = chips * (planes - 1)
    lax.fori_loop(0, own_place, greet, 0)
    lax.fori_loop(own_place + 1, chips * planes, greet, 0)
    pl.semaphore_signal(barrier, inc=1, device_id=sibling, device_id_type=MESH)

    lat_n = normed(lat_ref[...])
    query = (dot(lat_n, wq_ref[...]) * HD ** (-0.5)).astype(BF16)
    own_query[...] = query
    lat_rows = lat_ref.shape[0]
    lane = iota((1, 128), 1)
    low = lane < HD

    first_pos = (me_c * planes + me_h) * rows
    for half in range(2):
        span = near * 2 * lat_rows
        at = pl.ds(half * span, span)
        pos = jnp.transpose(jnp.broadcast_to(lpos_ref[:, at], (128, span))).reshape(near, 2, lat_rows, 128)
        for k in range(2):
            pos_k = pos[:, k].reshape(near * lat_rows, 128)
            for b in range(rows // BLOCK):
                hit = (kb_ref[...] == b) & (iota(kb_ref.shape, 1) < kc_ref[...])
                kept = jnp.max(jnp.where(hit, 1.0, 0.0), axis=1, keepdims=True)
                at_b = pl.ds(b * BLOCK, BLOCK)
                key_pos = jnp.where(kept > 0.5, first_pos + b * BLOCK + lane, FAR)
                bias[half * 2 + k, :, at_b] = jnp.where(key_pos < pos_k, 0.0, NEG_FILL)
    values[:, :, 128:] = jnp.ones(values.shape[:2] + (128,), BF16)

    pl.semaphore_wait(barrier, chips * planes)

    def q_slot(g, half, k):
        return pl.multiple_of(((g * 2 + half) * 2 + k) * near, near)

    own_slot = queries.at[q_slot(me_h, me_half, me_k) + lax.rem(me_p, near)]
    own_sem = q_recv.at[me_h * 2 + me_half]

    def send_query(i, carry):
        pltpu.make_async_remote_copy(
            src_ref=own_query, dst_ref=own_slot, send_sem=q_send, recv_sem=own_sem,
            device_id=peer(i), device_id_type=MESH,
        ).start()
        return carry

    lax.fori_loop(0, own_place, send_query, 0)
    pltpu.make_async_copy(own_query, own_slot, own_sem).start()
    lax.fori_loop(own_place + 1, chips * planes, send_query, 0)

    wk_copy.wait()
    wv_copy.wait()
    pairs = keys.shape[0]

    def project(t, carry):
        x_copy(t).wait()
        at = pl.ds(pl.multiple_of(t * tile, tile), tile)
        n = normed(x[at, :])
        k = dot(n, wk[...]).astype(BF16)
        for p in range(pairs):
            keys[p, at, :] = k[:, p * 128:(p + 1) * 128]
        v = dot(n, wv[...]).astype(BF16)
        for p in range(pairs):
            values[p, at, 0:128] = v[:, p * 128:(p + 1) * 128]
        return carry

    def groups(step):
        return lax.rem(me_h + 1 + step, planes), lax.rem(me_h + 2 * planes - 1 - step, planes)

    def forward(step):
        for half, g in enumerate(groups(step)):
            slots = queries.at[pl.ds(q_slot(g, half, me_k), near)]
            pltpu.make_async_copy(slots, slots, q_recv.at[g * 2 + half]).wait()
            pltpu.make_async_remote_copy(
                src_ref=slots, dst_ref=slots, send_sem=f_send, recv_sem=f_recv.at[g * 2 + half],
                device_id=sibling, device_id_type=MESH,
            ).start()

    def forwarded(step):
        for half, g in enumerate(groups(step)):
            slots = queries.at[pl.ds(q_slot(g, half, 1 - me_k), near)]
            pltpu.make_async_copy(slots, slots, f_recv.at[g * 2 + half]).wait()

    lax.fori_loop(0, rows // tile, project, 0)
    forward(0)
    forwarded(0)

    step_rows = near * lat_rows
    units = [(half, j) for half in range(2) for j in range(2)]
    chunk, part_rows = 256, 1024
    last = 2 * planes - 1

    def where_at(it):
        return lax.div(it, 2), lax.rem(me_k + 1 + it, 2)

    def load_query(it, unit):
        half, j = unit
        step, k = where_at(it)
        g = groups(step)[half]
        q = queries[pl.ds(q_slot(g, half, k), near), :, j * 128:(j + 1) * 128].reshape(step_rows, 128)
        zero = jnp.zeros_like(q)
        return jnp.concatenate([jnp.where(low, q, zero), jnp.where(low, zero, q)], 0), g * 2 + j, half * 2 + k

    def score(u, q, pair, tile_at, at, peak):
        s = lax.dot_general(q, keys[pair, at, :], (((1,), (1,)), ((), ())), preferred_element_type=F32)
        off = bias[tile_at, :, at]
        s = jnp.concatenate([s[:step_rows] + off, s[step_rows:] + off], 0)
        scores[u % 2, :, at] = s
        for i in range(chunk // 128):
            piece = s[:, i * 128:(i + 1) * 128]
            peak = piece if peak is None else jnp.maximum(peak, piece)
        return peak

    def top_of(peak):
        return jnp.broadcast_to(jnp.max(peak, axis=1, keepdims=True), peak.shape)

    peak = None
    loaded = load_query(0, units[0])
    for c in range(rows // chunk):
        peak = score(0, *loaded, pl.ds(c * chunk, chunk), peak)
    tops[...] = top_of(peak)

    def iteration(it, carry):
        step, _ = where_at(it)
        odd = lax.rem(it, 2)
        more = step < planes - 1

        @pl.when((odd == 0) & more)
        def _():
            forward(step + 1)

        @pl.when((odd == 1) & more)
        def _():
            forwarded(step + 1)

        here = groups(step)
        top = tops[...]
        stats = None
        for u in range(len(units)):
            nxt = u + 1
            if nxt < len(units):
                loaded = load_query(it, units[nxt])
            else:
                loaded = load_query(jnp.minimum(it + 1, last), units[0])
            half, j = units[u]
            peak = total = None
            for c in range(rows // chunk):
                at = pl.ds(c * chunk, chunk)
                peak = score(nxt, *loaded, at, peak)
                wide_top = jnp.concatenate([top] * (chunk // 128), 1)
                weights[:, at] = jnp.exp(scores[u % 2, :, at] - wide_top).astype(BF16)
                if (c + 1) * chunk % part_rows == 0:
                    at = pl.ds((c + 1) * chunk - part_rows, part_rows)
                    part = dot(weights[:, at], values[here[half] * 2 + j, at, :])
                    total = part if total is None else total + part
            both = jnp.where(low, total[:step_rows, :128], total[step_rows:, :128]).astype(BF16)
            own[it, half, :, :, j * 128:(j + 1) * 128] = both.reshape(near, lat_rows, 128)
            new = totals_of(lane, 2 * j, top[:step_rows], total[:step_rows, 128:])
            new = new + totals_of(lane, 2 * j + 1, top[step_rows:], total[step_rows:, 128:])
            if j == 0:
                stats = new
            else:
                own[it, half, :, :, 256:384] = (stats + new).astype(BF16).reshape(near, lat_rows, 128)
            top = top_of(peak)
        tops[...] = top

        @pl.when(odd == 0)
        def _():
            pltpu.make_async_remote_copy(
                src_ref=own.at[it], dst_ref=other.at[step], send_sem=o_send, recv_sem=o_recv.at[step],
                device_id=sibling, device_id_type=MESH,
            ).start()

        @pl.when(odd == 1)
        def _():
            pltpu.make_async_copy(other.at[step], other.at[step], o_recv.at[step]).wait()
            shape = own.shape[1:]
            flat = (shape[0] * shape[1] * shape[2], shape[3])
            weighted, stats = merge(own[it].reshape(flat), other[step].reshape(flat))
            merged[step, :, :, :, 0:256] = weighted.astype(BF16).reshape(shape[:3] + (256,))
            merged[step, :, :, :, 256:384] = stats.astype(BF16).reshape(shape[:3] + (128,))

            def send_part(i, carry):
                chip = lax.rem(me_p + i, chips)
                half = lax.div(chip, near)
                g = jnp.where(half == 0, here[0], here[1])
                pltpu.make_async_remote_copy(
                    src_ref=merged.at[step, half, lax.rem(chip, near)], dst_ref=arrived.at[me_h * chips + me_p],
                    send_sem=p_send, recv_sem=p_recv, device_id=(chip * 2 + me_k, g), device_id_type=MESH,
                ).start()
                return carry

            lax.fori_loop(lax.div(step + 1, planes), chips, send_part, 0)

        return carry

    lax.fori_loop(0, last + 1, iteration, 0)
    pltpu.make_async_copy(
        merged.at[planes - 1, me_half, lax.rem(me_p, near)], arrived.at[me_h * chips + me_p], p_recv
    ).start()

    width = wq_ref.shape[1]
    mine = pl.ds(pl.multiple_of(me_h * width, width), width)
    self_key = dot(lat_n, wk[:, mine]).astype(BF16)
    self_value = dot(lat_n, wv[:, mine]).astype(BF16).astype(F32)
    prod = query.astype(F32) * self_key.astype(F32)
    self_score = pick_dot(prod, iota((width, 128), 0) // HD == iota((width, 128), 1) % (width // HD))

    pltpu.make_async_copy(arrived, arrived, p_recv).wait()
    out_ref[...] = combine(arrived, self_score, self_value)
    sent = queries.at[pl.ds(0, chips * planes - 1)]
    pltpu.make_async_copy(sent, sent, q_send).wait()
    sent = queries.at[pl.ds(0, chips * planes)]
    pltpu.make_async_copy(sent, sent, f_send).wait()
    pltpu.make_async_copy(other, other, o_send).wait()
    sent = arrived.at[pl.ds(0, chips * planes - 1)]
    pltpu.make_async_copy(sent, sent, p_send).wait()


def per_device(prefix, keep_blocks, keep_count, latent_inputs, latent_pos, w_query, w_key, w_value):
    ctx_size, head_size = lax.axis_size("ctx"), lax.axis_size("head")
    rows, d = prefix.shape
    lat_rows, width = latent_inputs.shape[0], w_query.shape[1]
    latents, cols = lat_rows * ctx_size, width * head_size
    pairs = cols // 128
    shards = ctx_size * head_size
    near = ctx_size // 4
    wide = width + 128
    vmem = pl.BlockSpec(memory_space=pltpu.VMEM)
    hbm = pl.BlockSpec(memory_space=pl.ANY)
    dma = pltpu.SemaphoreType.DMA
    return pl.pallas_call(
        functools.partial(whole_kernel, (ctx_size, head_size)),
        in_specs=[vmem] * 5 + [hbm] * 3,
        out_specs=vmem,
        out_shape=jax.ShapeDtypeStruct((lat_rows, width), BF16),
        scratch_shapes=[
            pltpu.VMEM((rows, d), BF16),
            pltpu.VMEM((d, cols), BF16),
            pltpu.VMEM((d, cols), BF16),
            pltpu.VMEM((pairs, rows, 128), BF16),
            pltpu.VMEM((pairs, rows, 256), BF16),
            pltpu.VMEM((lat_rows, width), BF16),
            pltpu.VMEM((shards, lat_rows, width), BF16),
            pltpu.VMEM((4, latents // 4, rows), F32),
            pltpu.VMEM((2, 256, rows), F32),
            pltpu.VMEM((256, rows), BF16),
            pltpu.VMEM((256, 128), F32),
            pltpu.VMEM((2 * head_size, 2, near, lat_rows, wide), BF16),
            pltpu.VMEM((head_size, 2, near, lat_rows, wide), BF16),
            pltpu.VMEM((head_size, 2, near, lat_rows, wide), BF16),
            pltpu.VMEM((shards // 2, lat_rows, wide), BF16),
            dma((rows // 512,)),
            dma((2,)),
            dma,
            dma((2 * head_size,)),
            dma,
            dma((2 * head_size,)),
            dma,
            dma((head_size,)),
            dma,
            dma,
        ],
        name="whole",
        compiler_params=pltpu.CompilerParams(
            collective_id=0, has_side_effects=True, vmem_limit_bytes=60 << 20
        ),
        cost_estimate=pl.CostEstimate(
            flops=4 * rows * d * cols + 4 * latents * rows * cols,
            bytes_accessed=2 * rows * d + 4 * d * cols,
            transcendentals=latents * rows * 2 * pairs,
        ),
    )(
        latent_inputs, w_query, latent_pos.reshape(1, latents),
        keep_blocks.reshape(1, -1), keep_count.reshape(1, 1), prefix, w_key, w_value,
    )


def solution(mesh):
    return jax.shard_map(
        per_device,
        mesh=mesh,
        in_specs=(
            P(("ctx", "head"), None),
            P("head", "ctx", None),
            P("head", "ctx"),
            P("ctx", None),
            P(),
            P(None, "head"),
            P(),
            P(),
        ),
        out_specs=P("ctx", "head"),
        check_vma=False,
    )
```

time: 66.3 us -> 60.6 us (0.914)
  Pallas kernels: 62.7 us -> 58.5 us
  other arithmetic: 1.4 us -> 0 us
    pallas_call x1, Pallas kernels: 62.7 us -> 58.5 us  [per_device(): pl.pallas_call(functools.partial(whole_kernel, (ctx_size, head_size)), in...]
    reduce_or x1 -> x0, other arithmetic: 0.78 us -> none  [per_device(): kept = jnp.repeat(jnp.any(match, axis=1), BLOCK)]
    unnamed x2 -> x1, local copies, waits for them, and re-layouts: 1.37 us -> 1.3 us
where the time goes in v3:
time: 60.6 us; the launch traced here: 60.5 us
  Pallas kernels  58.5 us (97%)
  local copies, waits for them, and re-layouts  1.3 us (2%)
  between operations  0.66 us (1%)
    pallas_call x1, Pallas kernels, per_device(): pl.pallas_call(functools.partial(whole_kernel, (ctx_size, head_size)), in...  58.5 us
    unnamed x1, local copies, waits for them, and re-layouts  1.3 us

profile of v3, /device:TPU:1, one launch (start us, length us, event | category | flops | bytes accessed | tf_op | source)
XLA Modules:
  0.0 60.5 jit_solution(10167622151326657531)
XLA Ops:
  0.7 58.5 %whole.1 = bf16[16,256]{1,0:T(8,128)(2,1)} custom-call(bf16[16,1024]{1,0:T(8,128)(2,1)} %lat_ref.1, bf16[1024,256]{1,0:T(8,128)(2,1)} %wq_ref.1, s32[1,512]{1,0:T(1,128)} %bitcast.2, s32[1,16]{1,0:T(1,128)} %bitcast.3, s32[1,1]{1,0:T(1,128)S(6)} %copy.10.kc_ref, bf16[2048,1024]{1,0:T(8,128)(2,1)} %x_hbm.1, bf16[1024,1024]{1,0:T(8,128)(2,1)} %wk_hbm.1, ...), custom_call_target="tpu_custom_call" | custom-call | flops 12884901888 | bytes 8388608 | tf_op jit(solution)/shard_map/whole/pallas_call | solution.py:364
  59.2 1.3 %copy.11 = bf16[16,256]{1,0:T(8,128)(2,1)} copy(bf16[16,256]{1,0:T(8,128)(2,1)} %whole.1) | data formatting | bytes 16384

commit v4 on v3

--- a/solution.py
+++ b/solution.py
@@ -83,22 +83,24 @@
     return jnp.where(lane % 4 == head, pieces_of(lane, top, weight_sum), 0.0)
 
 
-def merge(mine, theirs):
-    rows, wide = mine.shape
-    both = jnp.concatenate([mine, theirs], 0)
+def merge(blocks):
+    rows, wide = blocks[0].shape
+    many = jnp.concatenate(blocks, 0)
     r, c = iota((128, 128), 0), iota((128, 128), 1)
-    tops = dot(both[:, 256:], ((r < 12) & (r % 4 == c % 4)).astype(BF16))
-    top = jnp.maximum(tops[:rows], tops[rows:])
-    scaled = both.astype(F32) * spread_scale(jnp.exp(tops - jnp.concatenate([top, top], 0)), wide)
-    total = scaled[:rows] + scaled[rows:]
+    tops = dot(many[:, 256:], ((r < 12) & (r % 4 == c % 4)).astype(BF16))
+    cut = lambda whole: [whole[i * rows:(i + 1) * rows] for i in range(len(blocks))]
+    top = functools.reduce(jnp.maximum, cut(tops))
+    scale = jnp.exp(tops - jnp.concatenate([top] * len(blocks), 0))
+    total = sum(cut(many.astype(F32) * spread_scale(scale, wide)))
     weight_sum = pick_dot(total[:, 256:], (r >= 12) & (r < 20) & (r % 4 == c % 4))
-    return total[:, :256], pieces_of(iota((1, 128), 1), top, weight_sum)
+    stats = pieces_of(iota((1, 128), 1), top, weight_sum)
+    return jnp.concatenate([total[:, :256], stats], 1).astype(BF16)
 
 
 def whole_kernel(
     sizes, lat_ref, wq_ref, lpos_ref, kb_ref, kc_ref, x_hbm, wk_hbm, wv_hbm, out_ref,
-    x, wk, wv, keys, values, own_query, queries, bias, scores, weights, tops, own, other, merged, arrived,
-    x_sem, w_sem, q_send, q_recv, f_send, f_recv, o_send, o_recv, p_send, p_recv,
+    x, wk, wv, keys, values, queries, plane_query, bias, scores, weights, tops, own, other, merged, along_z, arrived,
+    x_sem, w_sem, s_send, s_recv, q_send, q_recv, f_send, f_recv, o_send, o_recv, z_send, z_recv, p_send, p_recv,
 ):
     ctx_size, planes = sizes
     chips = ctx_size // 2
@@ -124,24 +126,28 @@
 
     barrier = pltpu.get_barrier_semaphore()
 
-    def peer(i):
-        away = 1 + lax.div(i, chips)
-        plane = lax.rem(jnp.where(me_half == 0, me_h + planes - away, me_h + away), planes)
-        chip = lax.rem(me_p + lax.rem(i, chips), chips)
-        return (chip * 2 + me_k, plane)
-
-    def greet(i, carry):
-        pl.semaphore_signal(barrier, inc=1, device_id=peer(i), device_id_type=MESH)
+    def in_plane(away):
+        return (me_c, lax.rem(me_h + away, planes))
+
+    def in_chip(away):
+        return (lax.rem(me_p + away, chips) * 2 + me_k, me_h)
+
+    def greet(device):
+        pl.semaphore_signal(barrier, inc=1, device_id=device, device_id_type=MESH)
+
+    for away in range(1, planes):
+        greet(in_plane(away))
+    greet(sibling)
+
+    def greet_chip(away, carry):
+        greet(in_chip(away))
         return carry
 
-    own_place = chips * (planes - 1)
-    lax.fori_loop(0, own_place, greet, 0)
-    lax.fori_loop(own_place + 1, chips * planes, greet, 0)
-    pl.semaphore_signal(barrier, inc=1, device_id=sibling, device_id_type=MESH)
+    lax.fori_loop(1, chips, greet_chip, 0)
 
     lat_n = normed(lat_ref[...])
     query = (dot(lat_n, wq_ref[...]) * HD ** (-0.5)).astype(BF16)
-    own_query[...] = query
+    plane_query[me_h] = query
     lat_rows = lat_ref.shape[0]
     lane = iota((1, 128), 1)
     low = lane < HD
@@ -161,25 +167,6 @@
                 bias[half * 2 + k, :, at_b] = jnp.where(key_pos < pos_k, 0.0, NEG_FILL)
     values[:, :, 128:] = jnp.ones(values.shape[:2] + (128,), BF16)
 
-    pl.semaphore_wait(barrier, chips * planes)
-
-    def q_slot(g, half, k):
-        return pl.multiple_of(((g * 2 + half) * 2 + k) * near, near)
-
-    own_slot = queries.at[q_slot(me_h, me_half, me_k) + lax.rem(me_p, near)]
-    own_sem = q_recv.at[me_h * 2 + me_half]
-
-    def send_query(i, carry):
-        pltpu.make_async_remote_copy(
-            src_ref=own_query, dst_ref=own_slot, send_sem=q_send, recv_sem=own_sem,
-            device_id=peer(i), device_id_type=MESH,
-        ).start()
-        return carry
-
-    lax.fori_loop(0, own_place, send_query, 0)
-    pltpu.make_async_copy(own_query, own_slot, own_sem).start()
-    lax.fori_loop(own_place + 1, chips * planes, send_query, 0)
-
     wk_copy.wait()
     wv_copy.wait()
     pairs = keys.shape[0]
@@ -199,28 +186,60 @@
     def groups(step):
         return lax.rem(me_h + 1 + step, planes), lax.rem(me_h + 2 * planes - 1 - step, planes)
 
-    def forward(step):
-        for half, g in enumerate(groups(step)):
-            slots = queries.at[pl.ds(q_slot(g, half, me_k), near)]
-            pltpu.make_async_copy(slots, slots, q_recv.at[g * 2 + half]).wait()
+    def send_along_z():
+        for away in range(1, planes):
+            mine = plane_query.at[me_h]
             pltpu.make_async_remote_copy(
-                src_ref=slots, dst_ref=slots, send_sem=f_send, recv_sem=f_recv.at[g * 2 + half],
-                device_id=sibling, device_id_type=MESH,
+                src_ref=mine, dst_ref=mine, send_sem=s_send, recv_sem=s_recv,
+                device_id=in_plane(away), device_id_type=MESH,
             ).start()
+
+    def send_in_plane():
+        some = plane_query.at[pl.ds(0, planes - 1)]
+        pltpu.make_async_copy(some, some, s_recv).wait()
+        slots = queries.at[:, me_half, me_k, lax.rem(me_p, near)]
+
+        def send(away, carry):
+            pltpu.make_async_remote_copy(
+                src_ref=plane_query, dst_ref=slots, send_sem=q_send, recv_sem=q_recv,
+                device_id=in_chip(away), device_id_type=MESH,
+            ).start()
+            return carry
+
+        lax.fori_loop(1, chips, send, 0)
+        pltpu.make_async_copy(plane_query, slots, q_recv).start()
+
+    def forward():
+        mine = queries.at[:, :, me_k]
+        pltpu.make_async_copy(mine, mine, q_recv).wait()
+        for step in range(planes):
+            for half, g in enumerate(groups(step)):
+                slots = queries.at[g, half, me_k]
+                pltpu.make_async_remote_copy(
+                    src_ref=slots, dst_ref=slots, send_sem=f_send, recv_sem=f_recv.at[g * 2 + half],
+                    device_id=sibling, device_id_type=MESH,
+                ).start()
 
     def forwarded(step):
         for half, g in enumerate(groups(step)):
-            slots = queries.at[pl.ds(q_slot(g, half, 1 - me_k), near)]
+            slots = queries.at[g, half, 1 - me_k]
             pltpu.make_async_copy(slots, slots, f_recv.at[g * 2 + half]).wait()
 
-    lax.fori_loop(0, rows // tile, project, 0)
-    forward(0)
+    project(0, 0)
+    pl.semaphore_wait(barrier, chips - 1 + planes)
+    send_along_z()
+    project(1, 0)
+    send_in_plane()
+    lax.fori_loop(2, rows // tile, project, 0)
+    forward()
     forwarded(0)
 
     step_rows = near * lat_rows
     units = [(half, j) for half in range(2) for j in range(2)]
     chunk, part_rows = 256, 1024
     last = 2 * planes - 1
+    block = own.shape[1:]
+    flat = (block[0] * block[1] * block[2], block[3])
 
     def where_at(it):
         return lax.div(it, 2), lax.rem(me_k + 1 + it, 2)
@@ -229,7 +248,7 @@
         half, j = unit
         step, k = where_at(it)
         g = groups(step)[half]
-        q = queries[pl.ds(q_slot(g, half, k), near), :, j * 128:(j + 1) * 128].reshape(step_rows, 128)
+        q = queries[g, half, k, :, :, j * 128:(j + 1) * 128].reshape(step_rows, 128)
         zero = jnp.zeros_like(q)
         return jnp.concatenate([jnp.where(low, q, zero), jnp.where(low, zero, q)], 0), g * 2 + j, half * 2 + k
 
@@ -256,10 +275,6 @@
         step, _ = where_at(it)
         odd = lax.rem(it, 2)
         more = step < planes - 1
-
-        @pl.when((odd == 0) & more)
-        def _():
-            forward(step + 1)
 
         @pl.when((odd == 1) & more)
         def _():
@@ -303,33 +318,37 @@
                 device_id=sibling, device_id_type=MESH,
             ).start()
 
-        @pl.when(odd == 1)
+        @pl.when((odd == 1) & more)
         def _():
             pltpu.make_async_copy(other.at[step], other.at[step], o_recv.at[step]).wait()
-            shape = own.shape[1:]
-            flat = (shape[0] * shape[1] * shape[2], shape[3])
-            weighted, stats = merge(own[it].reshape(flat), other[step].reshape(flat))
-            merged[step, :, :, :, 0:256] = weighted.astype(BF16).reshape(shape[:3] + (256,))
-            merged[step, :, :, :, 256:384] = stats.astype(BF16).reshape(shape[:3] + (128,))
-
-            def send_part(i, carry):
-                chip = lax.rem(me_p + i, chips)
-                half = lax.div(chip, near)
-                g = jnp.where(half == 0, here[0], here[1])
+            merged[step] = merge([own[it].reshape(flat), other[step].reshape(flat)]).reshape(block)
+            for half, g in enumerate(here):
                 pltpu.make_async_remote_copy(
-                    src_ref=merged.at[step, half, lax.rem(chip, near)], dst_ref=arrived.at[me_h * chips + me_p],
-                    send_sem=p_send, recv_sem=p_recv, device_id=(chip * 2 + me_k, g), device_id_type=MESH,
+                    src_ref=merged.at[step, half], dst_ref=along_z.at[step, half],
+                    send_sem=z_send, recv_sem=z_recv.at[step], device_id=(me_c, g), device_id_type=MESH,
                 ).start()
-                return carry
-
-            lax.fori_loop(lax.div(step + 1, planes), chips, send_part, 0)
 
         return carry
 
     lax.fori_loop(0, last + 1, iteration, 0)
-    pltpu.make_async_copy(
-        merged.at[planes - 1, me_half, lax.rem(me_p, near)], arrived.at[me_h * chips + me_p], p_recv
-    ).start()
+
+    final = planes - 1
+    pltpu.make_async_copy(other.at[final], other.at[final], o_recv.at[final]).wait()
+    for step in range(planes - 1):
+        pltpu.make_async_copy(along_z.at[step], along_z.at[step], z_recv.at[step]).wait()
+    blocks = [own[last], other[final]] + [along_z[step] for step in range(planes - 1)]
+    merged[final] = merge([one.reshape(flat) for one in blocks]).reshape(block)
+
+    def send_part(away, carry):
+        chip = lax.rem(me_p + away, chips)
+        pltpu.make_async_remote_copy(
+            src_ref=merged.at[final, lax.div(chip, near), lax.rem(chip, near)], dst_ref=arrived.at[me_p],
+            send_sem=p_send, recv_sem=p_recv, device_id=in_chip(away), device_id_type=MESH,
+        ).start()
+        return carry
+
+    lax.fori_loop(1, chips, send_part, 0)
+    pltpu.make_async_copy(merged.at[final, me_half, lax.rem(me_p, near)], arrived.at[me_p], p_recv).start()
 
     width = wq_ref.shape[1]
     mine = pl.ds(pl.multiple_of(me_h * width, width), width)
@@ -340,12 +359,15 @@
 
     pltpu.make_async_copy(arrived, arrived, p_recv).wait()
     out_ref[...] = combine(arrived, self_score, self_value)
-    sent = queries.at[pl.ds(0, chips * planes - 1)]
+    sent = plane_query.at[pl.ds(0, planes - 1)]
+    pltpu.make_async_copy(sent, sent, s_send).wait()
+    sent = values.at[0, pl.ds(0, (chips - 1) * planes * lat_rows)]
     pltpu.make_async_copy(sent, sent, q_send).wait()
-    sent = queries.at[pl.ds(0, chips * planes)]
+    sent = queries.at[:, :, 0]
     pltpu.make_async_copy(sent, sent, f_send).wait()
     pltpu.make_async_copy(other, other, o_send).wait()
-    sent = arrived.at[pl.ds(0, chips * planes - 1)]
+    pltpu.make_async_copy(along_z, along_z, z_send).wait()
+    sent = arrived.at[pl.ds(0, chips - 1)]
     pltpu.make_async_copy(sent, sent, p_send).wait()
 
 
@@ -355,7 +377,6 @@
     lat_rows, width = latent_inputs.shape[0], w_query.shape[1]
     latents, cols = lat_rows * ctx_size, width * head_size
     pairs = cols // 128
-    shards = ctx_size * head_size
     near = ctx_size // 4
     wide = width + 128
     vmem = pl.BlockSpec(memory_space=pltpu.VMEM)
@@ -372,8 +393,8 @@
             pltpu.VMEM((d, cols), BF16),
             pltpu.VMEM((pairs, rows, 128), BF16),
             pltpu.VMEM((pairs, rows, 256), BF16),
-            pltpu.VMEM((lat_rows, width), BF16),
-            pltpu.VMEM((shards, lat_rows, width), BF16),
+            pltpu.VMEM((head_size, 2, 2, near, lat_rows, width), BF16),
+            pltpu.VMEM((head_size, lat_rows, width), BF16),
             pltpu.VMEM((4, latents // 4, rows), F32),
             pltpu.VMEM((2, 256, rows), F32),
             pltpu.VMEM((256, rows), BF16),
@@ -381,15 +402,20 @@
             pltpu.VMEM((2 * head_size, 2, near, lat_rows, wide), BF16),
             pltpu.VMEM((head_size, 2, near, lat_rows, wide), BF16),
             pltpu.VMEM((head_size, 2, near, lat_rows, wide), BF16),
-            pltpu.VMEM((shards // 2, lat_rows, wide), BF16),
+            pltpu.VMEM((head_size - 1, 2, near, lat_rows, wide), BF16),
+            pltpu.VMEM((ctx_size // 2, lat_rows, wide), BF16),
             dma((rows // 512,)),
             dma((2,)),
             dma,
+            dma,
+            dma,
+            dma,
+            dma,
             dma((2 * head_size,)),
             dma,
-            dma((2 * head_size,)),
-            dma,
             dma((head_size,)),
+            dma,
+            dma((head_size - 1,)),
             dma,
             dma,
         ],

time: 60.6 us -> 57.6 us (0.950)
  Pallas kernels: 58.5 us -> 55.5 us
    pallas_call x1, Pallas kernels: 58.5 us -> 55.5 us  [per_device(): pl.pallas_call(functools.partial(whole_kernel, (ctx_size, head_size)), in...]
where the time goes in v4:
time: 57.6 us; the launch traced here: 57.5 us
  Pallas kernels  55.5 us (96%)
  local copies, waits for them, and re-layouts  1.3 us (2%)
  between operations  0.66 us (1%)
    pallas_call x1, Pallas kernels, per_device(): pl.pallas_call(functools.partial(whole_kernel, (ctx_size, head_size)), in...  55.5 us
    unnamed x1, local copies, waits for them, and re-layouts  1.3 us

profile of v4, /device:TPU:1, one launch (start us, length us, event | category | flops | bytes accessed | tf_op | source)
XLA Modules:
  0.0 57.5 jit_solution(7871277460050213666)
XLA Ops:
  0.7 55.5 %whole.1 = bf16[16,256]{1,0:T(8,128)(2,1)} custom-call(bf16[16,1024]{1,0:T(8,128)(2,1)} %lat_ref.1, bf16[1024,256]{1,0:T(8,128)(2,1)} %wq_ref.1, s32[1,512]{1,0:T(1,128)} %bitcast.2, s32[1,16]{1,0:T(1,128)} %bitcast.3, s32[1,1]{1,0:T(1,128)S(6)} %copy.10.kc_ref, bf16[2048,1024]{1,0:T(8,128)(2,1)} %x_hbm.1, bf16[1024,1024]{1,0:T(8,128)(2,1)} %wk_hbm.1, ...), custom_call_target="tpu_custom_call" | custom-call | flops 12884901888 | bytes 8388608 | tf_op jit(solution)/shard_map/whole/pallas_call | solution.py:385
  56.2 1.3 %copy.11 = bf16[16,256]{1,0:T(8,128)(2,1)} copy(bf16[16,256]{1,0:T(8,128)(2,1)} %whole.1) | data formatting | bytes 16384

commit v5 on v4

--- a/solution.py
+++ b/solution.py
@@ -44,31 +44,36 @@
     return high, x - high
 
 
-def spread_scale(scale, wide):
-    high, rest = split_two(scale)
+def spread(value):
+    high, rest = split_two(value)
     lane = iota((1, 128), 1)
     pieces = jnp.where(lane < 4, high, jnp.where(lane < 8, rest, 0.0)).astype(BF16)
-    r, c = iota((128, wide), 0), iota((128, wide), 1)
-    head = jnp.where(c < 256, c // HD, jnp.where((c >= 268) & (c < 276), c % 4, 4))
-    return dot(pieces, ((r < 8) & (r % 4 == head)).astype(BF16))
+    r, c = iota((128, 256), 0), iota((128, 256), 1)
+    return dot(pieces, ((r < 8) & (r % 4 == c // HD)).astype(BF16))
+
+
+def read_totals(stats):
+    r, c = iota((128, 256), 0), iota((128, 256), 1)
+    piece = jnp.where(c < 128, (r < 12).astype(jnp.int32), ((r >= 12) & (r < 20)).astype(jnp.int32))
+    both = dot(stats, ((piece == 1) & (r % 4 == c % 4)).astype(BF16))
+    return both[:, :128], both[:, 128:]
 
 
 def combine(parts_ref, own, self_value):
     shards, rows, wide = parts_ref.shape
     parts = parts_ref[...]
-    stats = parts[:, :, 256:].reshape(shards * rows, 128)
-    r, c = iota((128, 128), 0), iota((128, 128), 1)
-    join = ((r < 12) & (r % 4 == c % 4)).astype(BF16)
-    tops = dot(stats, join).reshape(shards, rows, 128)
+    tops, sums = read_totals(parts[:, :, 256:].reshape(shards * rows, 128))
+    tops = tops.reshape(shards, rows, 128)
     top = jnp.maximum(jnp.max(tops, axis=0), own)
-    scale = jnp.exp(tops - top[None]).reshape(shards * rows, 128)
-    scales = spread_scale(scale, wide).reshape(shards, rows, wide)
-    total = jnp.sum(scales * parts.astype(F32), axis=0)
-    r, c = iota((128, 256), 0), iota((128, 256), 1)
-    denominator = pick_dot(total[:, 256:], ((r >= 12) & (r < 20) & (r % 4 == c // HD)).astype(F32))
-    self_weight = pick_dot(jnp.exp(own - top), ((r < 4) & (r == c // HD)).astype(F32))
-    numerator = total[:, :256] + self_weight * self_value
-    return (numerator / (denominator + self_weight)).astype(BF16)
+    scale = jnp.exp(tops - top[None])
+    self_weight = jnp.exp(own - top)
+    denominator = jnp.sum(scale * sums.reshape(shards, rows, 128), axis=0) + self_weight
+    wanted = jnp.concatenate([scale.reshape(shards * rows, 128), self_weight, 1.0 / denominator], 0)
+    spreads = spread(wanted)
+    scales = spreads[: shards * rows].reshape(shards, rows, 256)
+    numerator = jnp.sum(scales * parts[:, :, :256].astype(F32), axis=0)
+    numerator = numerator + spreads[shards * rows : shards * rows + rows] * self_value
+    return (numerator * spreads[shards * rows + rows :]).astype(BF16)
 
 
 def pieces_of(lane, top, weight_sum):
@@ -84,17 +89,15 @@
 
 
 def merge(blocks):
-    rows, wide = blocks[0].shape
+    rows = blocks[0].shape[0]
     many = jnp.concatenate(blocks, 0)
-    r, c = iota((128, 128), 0), iota((128, 128), 1)
-    tops = dot(many[:, 256:], ((r < 12) & (r % 4 == c % 4)).astype(BF16))
     cut = lambda whole: [whole[i * rows:(i + 1) * rows] for i in range(len(blocks))]
+    tops, sums = read_totals(many[:, 256:])
     top = functools.reduce(jnp.maximum, cut(tops))
     scale = jnp.exp(tops - jnp.concatenate([top] * len(blocks), 0))
-    total = sum(cut(many.astype(F32) * spread_scale(scale, wide)))
-    weight_sum = pick_dot(total[:, 256:], (r >= 12) & (r < 20) & (r % 4 == c % 4))
-    stats = pieces_of(iota((1, 128), 1), top, weight_sum)
-    return jnp.concatenate([total[:, :256], stats], 1).astype(BF16)
+    total = sum(cut(many[:, :256].astype(F32) * spread(scale)))
+    stats = pieces_of(iota((1, 128), 1), top, sum(cut(scale * sums)))
+    return jnp.concatenate([total, stats], 1).astype(BF16)
 
 
 def whole_kernel(
@@ -225,12 +228,11 @@
             slots = queries.at[g, half, 1 - me_k]
             pltpu.make_async_copy(slots, slots, f_recv.at[g * 2 + half]).wait()
 
-    project(0, 0)
     pl.semaphore_wait(barrier, chips - 1 + planes)
     send_along_z()
-    project(1, 0)
+    project(0, 0)
     send_in_plane()
-    lax.fori_loop(2, rows // tile, project, 0)
+    lax.fori_loop(1, rows // tile, project, 0)
     forward()
     forwarded(0)
 

time: 57.6 us -> 55.1 us (0.957)
  Pallas kernels: 55.5 us -> 53 us
    pallas_call x1, Pallas kernels: 55.5 us -> 53 us  [per_device(): pl.pallas_call(functools.partial(whole_kernel, (ctx_size, head_size)), in...]
where the time goes in v5:
time: 55.1 us; the launch traced here: 54.9 us
  Pallas kernels  53 us (96%)
  local copies, waits for them, and re-layouts  1.3 us (2%)
  between operations  0.66 us (1%)
    pallas_call x1, Pallas kernels, per_device(): pl.pallas_call(functools.partial(whole_kernel, (ctx_size, head_size)), in...  53 us
    unnamed x1, local copies, waits for them, and re-layouts  1.3 us

profile of v5, /device:TPU:1, one launch (start us, length us, event | category | flops | bytes accessed | tf_op | source)
XLA Modules:
  0.0 54.9 jit_solution(4715192384523650783)
XLA Ops:
  0.7 53.0 %whole.1 = bf16[16,256]{1,0:T(8,128)(2,1)} custom-call(bf16[16,1024]{1,0:T(8,128)(2,1)} %lat_ref.1, bf16[1024,256]{1,0:T(8,128)(2,1)} %wq_ref.1, s32[1,512]{1,0:T(1,128)} %bitcast.2, s32[1,16]{1,0:T(1,128)} %bitcast.3, s32[1,1]{1,0:T(1,128)S(6)} %copy.10.kc_ref, bf16[2048,1024]{1,0:T(8,128)(2,1)} %x_hbm.1, bf16[1024,1024]{1,0:T(8,128)(2,1)} %wk_hbm.1, ...), custom_call_target="tpu_custom_call" | custom-call | flops 12884901888 | bytes 8388608 | tf_op jit(solution)/shard_map/whole/pallas_call | solution.py:387
  53.6 1.3 %copy.11 = bf16[16,256]{1,0:T(8,128)(2,1)} copy(bf16[16,256]{1,0:T(8,128)(2,1)} %whole.1) | data formatting | bytes 16384

commit v6 on v5

--- a/solution.py
+++ b/solution.py
@@ -209,7 +209,8 @@
             ).start()
             return carry
 
-        lax.fori_loop(1, chips, send, 0)
+        for away in range(1, chips):
+            send(away, 0)
         pltpu.make_async_copy(plane_query, slots, q_recv).start()
 
     def forward():
@@ -349,7 +350,8 @@
         ).start()
         return carry
 
-    lax.fori_loop(1, chips, send_part, 0)
+    for away in range(1, chips):
+        send_part(away, 0)
     pltpu.make_async_copy(merged.at[final, me_half, lax.rem(me_p, near)], arrived.at[me_p], p_recv).start()
 
     width = wq_ref.shape[1]

time: 55.1 us -> 55.1 us (level)
  no operation moved by 1% of the time
where the time goes in v6:
time: 55.1 us; the launch traced here: 54.9 us
  Pallas kernels  52.9 us (96%)
  local copies, waits for them, and re-layouts  1.3 us (2%)
  between operations  0.66 us (1%)
    pallas_call x1, Pallas kernels, per_device(): pl.pallas_call(functools.partial(whole_kernel, (ctx_size, head_size)), in...  52.9 us
    unnamed x1, local copies, waits for them, and re-layouts  1.3 us

profile of v6, /device:TPU:1, one launch (start us, length us, event | category | flops | bytes accessed | tf_op | source)
XLA Modules:
  0.0 54.9 jit_solution(4695365222345765818)
XLA Ops:
  0.7 52.9 %whole.1 = bf16[16,256]{1,0:T(8,128)(2,1)} custom-call(bf16[16,1024]{1,0:T(8,128)(2,1)} %lat_ref.1, bf16[1024,256]{1,0:T(8,128)(2,1)} %wq_ref.1, s32[1,512]{1,0:T(1,128)} %bitcast.2, s32[1,16]{1,0:T(1,128)} %bitcast.3, s32[1,1]{1,0:T(1,128)S(6)} %copy.10.kc_ref, bf16[2048,1024]{1,0:T(8,128)(2,1)} %x_hbm.1, bf16[1024,1024]{1,0:T(8,128)(2,1)} %wk_hbm.1, ...), custom_call_target="tpu_custom_call" | custom-call | flops 12884901888 | bytes 8388608 | tf_op jit(solution)/shard_map/whole/pallas_call | solution.py:389
  53.6 1.3 %copy.11 = bf16[16,256]{1,0:T(8,128)(2,1)} copy(bf16[16,256]{1,0:T(8,128)(2,1)} %whole.1) | data formatting | bytes 16384
